TPU v7x, 256 devices: a whole 4x4x8 slice. The times are simulated.
256 devices in a mesh: row: 8 (over z_lo, y), col: 4 (over z_hi), depth: 8 (over x, core).
Axes of the slice: x: 4, y: 4, z: 8 (z_hi: 4, z_lo: 2; z = z_hi * 2 + z_lo), core: 2. Of those that a mesh axis runs over, the one named last changes fastest.
Arguments:
- tokens: bfloat16 [2048, 12288], P(('row', 'col'), 'depth'), may hold values from -6 to 6
- weight: bfloat16 [12288, 24576], P('depth', ('row', 'col')), may hold values from -5 to 5
- moment: bfloat16 [12288, 24576], P('depth', ('row', 'col')), may hold values from -0.59765625 to 0.59765625
- upstream: bfloat16 [8, 256, 24576], P(None, 'col', ('row', 'depth')), may hold values from -24 to 24
Outputs:
- activated: bfloat16 [8, 256, 24576], P(None, 'col', ('row', 'depth'))
- new_weight: bfloat16 [12288, 24576], P('depth', ('row', 'col'))
- new_moment: bfloat16 [12288, 24576], P('depth', ('row', 'col'))
All inputs are finite; a program needn't handle non-finite values.
Results may differ from a plain program's by a relative error of at most 0.015.
Values may be sent and summed in bfloat16 or wider, within the bound.
A program may use at most 64 MiB of HBM per device.

v0:
```python
import jax
import jax.numpy as jnp
from jax import lax
from jax.sharding import PartitionSpec as P

D = 12288


gelu_coef = 0.7978845608028654
cubic_coef = 0.044715
lion_rate = 0.5
decay_rate = 0.1
beta_one = 0.9
beta_two = 0.99
smooth_tau = 0.1


def gelu_pair(preact):
    tangent = jnp.tanh(gelu_coef * (preact + cubic_coef * preact * preact * preact))
    gelu_value = 0.5 * preact * (1.0 + tangent)
    gelu_slope = 0.5 * (1.0 + tangent) + 0.5 * preact * (1.0 - tangent * tangent) * gelu_coef * (
        1.0 + 3.0 * cubic_coef * preact * preact
    )
    return (gelu_value, gelu_slope)


def shards(tokens, weight, moment, upstream):
    row_count = lax.axis_size("row")
    tok_rows = tokens.shape[0]
    fan_scale = D ** (-0.5)
    gathered = lax.all_gather(tokens, "row", axis=0, tiled=True)
    partial_value = jnp.dot(
        gathered,
        lax.all_gather(weight, "col", axis=1, tiled=True),
        preferred_element_type=jnp.float32,
    )
    summed = lax.psum_scatter(
        partial_value.astype(jnp.bfloat16), "depth", scatter_dimension=1, tiled=True
    ).astype(jnp.float32)
    gelu_value, gelu_slope = gelu_pair(summed * fan_scale)
    activated = gelu_value.astype(jnp.bfloat16)
    upstream_flat = upstream.reshape(row_count * tok_rows, upstream.shape[2]).astype(jnp.float32)
    local_grad = (upstream_flat * gelu_slope).astype(jnp.bfloat16)
    act_grad = lax.all_gather(local_grad, "depth", axis=1, tiled=True)
    grad_panel = lax.dot_general(
        gathered, act_grad, (((0,), (0,)), ((), ())), preferred_element_type=jnp.float32
    )
    grad_sum = lax.psum_scatter(
        grad_panel.astype(jnp.bfloat16), "col", scatter_dimension=1, tiled=True
    ).astype(jnp.float32)
    grad_full = grad_sum * fan_scale
    moment_f = moment.astype(jnp.float32)
    weight_f = weight.astype(jnp.float32)
    blended = beta_one * moment_f + (1.0 - beta_one) * grad_full
    update = blended / jnp.sqrt(blended * blended + smooth_tau * smooth_tau)
    new_weight = (weight_f - lion_rate * (update + decay_rate * weight_f)).astype(jnp.bfloat16)
    new_moment = (beta_two * moment_f + (1.0 - beta_two) * grad_full).astype(jnp.bfloat16)
    activated = activated.reshape(upstream.shape[0], upstream.shape[1], activated.shape[1])
    return (activated, new_weight, new_moment)


def solution(mesh):
    placed = (
        P(("row", "col"), "depth"),
        P("depth", ("row", "col")),
        P("depth", ("row", "col")),
        P(None, "col", ("row", "depth")),
    )
    return jax.shard_map(
        shards,
        mesh=mesh,
        in_specs=placed,
        out_specs=(
            P(None, "col", ("row", "depth")),
            P("depth", ("row", "col")),
            P("depth", ("row", "col")),
        ),
        check_vma=False,
    )
```

profile of v0, /device:TPU:1, one launch (start us, length us, event | category | flops | bytes accessed | tf_op | source)
XLA Modules:
  0.0 508.5 jit_solution(10022676626198729526)
XLA Ops:
  7.2 0.0 all-gather.4.cloned.1.call-start
  7.2 0.7 all-gather.4.cloned.1.call-update
  7.9 0.0 all-gather.6.cloned.1.call-start
  7.9 0.7 all-gather.6.cloned.1.call-update
  8.6 0.0 reduce-scatter.7.cloned.1.call-start
  8.7 41.9 %all-gather.4.cloned.1.call-done = bf16[512,1536]{1,0:T(8,128)(2,1)} async-done(((bf16[64,1536]{1,0:T(8,128)(2,1)}), bf16[512,1536]{1,0:T(8,128)(2,1)}) %all-gather.4.cloned.1.call-update) | async-done | bytes 1572880 | tf_op jit(solution)/shard_map/all_gather | solution.py:31
  50.6 180.1 %all-gather.6.cloned.1.call-done = bf16[1536,3072]{1,0:T(8,128)(2,1)} async-done(((bf16[1536,768]{1,0:T(8,128)(2,1)}), bf16[1536,3072]{1,0:T(8,128)(2,1)}) %all-gather.6.cloned.1.call-update) | async-done | bytes 9437200 | tf_op jit(solution)/shard_map/all_gather | solution.py:34
  230.8 8.1 %convolution_convert_fusion.1 = bf16[512,3072]{1,0:T(8,128)(2,1)S(1)} fusion(bf16[512,1536]{1,0:T(8,128)(2,1)} %all-gather.4.cloned.1.call-done, bf16[1536,3072]{1,0:T(8,128)(2,1)} %all-gather.6.cloned.1.call-done), kind=kOutput, calls=%fused_computation.14 | convolution fusion | flops 4833411072 | bytes 14155776 | tf_op jit(solution)/shard_map/dot_general | solution.py:32
  238.8 0.0 copy-start.3
  238.8 2.8 copy.15
  241.7 0.0 copy-start.4
  241.7 0.0 reduce-scatter.7.cloned.1.call-update
  241.7 0.0 all-gather.8.cloned.1.call-start
  241.7 34.0 %reduce-scatter.7.cloned.1.call-done = bf16[384,512]{1,0:T(8,128)(2,1)} async-done(((bf16[3072,512]{1,0:T(8,128)(2,1)}), bf16[384,512]{1,0:T(8,128)(2,1)}) %reduce-scatter.7.cloned.1.call-update) | async-done | bytes 393232
  275.8 1.2 copy.16
  277.0 0.0 copy-done.3
  277.0 1.5 fusion.18
  278.5 0.0 all-gather.8.cloned.1.call-update
  278.6 0.0 reduce-scatter.5.cloned.1.call-start
  278.6 32.4 %all-gather.8.cloned.1.call-done = bf16[512,3072]{1,0:T(8,128)(2,1)} async-done(((bf16[512,384]{1,0:T(8,128)(2,1)}), bf16[512,3072]{1,0:T(8,128)(2,1)}) %all-gather.8.cloned.1.call-update) | async-done | bytes 3145744 | tf_op jit(solution)/shard_map/all_gather | solution.py:44
  311.0 0.0 copy-done.4
  311.0 9.6 %fusion = bf16[1536,3072]{0,1:T(8,128)(2,1)} fusion(bf16[512,3072]{1,0:T(8,128)(2,1)} %all-gather.8.cloned.1.call-done, bf16[512,1536]{1,0:T(8,128)(2,1)S(1)} %copy-done.4), kind=kOutput, calls=%fused_computation.1 | convolution fusion | flops 4836556800 | bytes 14155776 | tf_op jit(solution)/shard_map/dot_general | solution.py:45
  320.6 0.0 copy-start
  320.6 0.0 reduce-scatter.5.cloned.1.call-update
  320.6 1.6 copy-done
  322.2 2.4 copy.11
  324.7 0.0 copy-start.1
  324.7 4.4 copy.12
  329.1 160.2 %reduce-scatter.5.cloned.1.call-done = bf16[1536,768]{0,1:T(8,128)(2,1)} async-done(((bf16[1536,3072]{0,1:T(8,128)(2,1)}), bf16[1536,768]{0,1:T(8,128)(2,1)}) %reduce-scatter.5.cloned.1.call-update) | async-done | bytes 2359312 | tf_op jit(solution)/shard_map/reduce_scatter | solution.py:48
  489.3 0.0 copy-done.1
  489.3 5.9 %fusion.6 = (bf16[1536,768]{0,1:T(8,128)(2,1)}, bf16[1536,768]{0,1:T(8,128)(2,1)}) fusion(bf16[1536,768]{0,1:T(8,128)(2,1)} %copy.12, bf16[1536,768]{0,1:T(8,128)(2,1)} %reduce-scatter.5.cloned.1.call-done, bf16[1536,768]{0,1:T(8,128)(2,1)S(1)} %copy-done.1), kind=kLoop, calls=%fused_computation.13 | loop fusion | flops 21233664 | bytes 11796480 | tf_op jit(solution)/shard_map/convert_element_type | solution.py:57
  495.1 0.0 copy-start.2
  495.1 4.4 copy.13
  499.5 0.0 copy-done.2
  499.5 2.4 copy.14
Async XLA Ops:
  7.2 43.5 %all-gather.4.cloned.1.call-start = ((), (), s32[]{:S(2)}) async-start(), calls=%async_computation.2 | async-start | bytes 1769472 | tf_op jit(solution)/shard_map/all_gather | solution.py:31
  7.9 222.9 %all-gather.6.cloned.1.call-start = ((), (), s32[]{:S(2)}) async-start(), calls=%async_computation.3 | async-start | bytes 11796480 | tf_op jit(solution)/shard_map/all_gather | solution.py:34
  8.6 267.1 %reduce-scatter.7.cloned.1.call-start = ((), (), s32[]{:S(2)}) async-start(), calls=%async_computation.6 | async-start | bytes 3538944
  238.8 38.1 %copy-start.3 = (bf16[8,64,384]{2,1,0:T(8,128)(2,1)S(1)}, bf16[8,64,384]{2,1,0:T(8,128)(2,1)}, u32[]{:S(2)}) copy-start(bf16[8,64,384]{2,1,0:T(8,128)(2,1)} %param.7) | copy-start | bytes 1179652
  241.7 69.3 %copy-start.4 = (bf16[512,1536]{1,0:T(8,128)(2,1)S(1)}, bf16[512,1536]{1,0:T(8,128)(2,1)}, u32[]{:S(2)}) copy-start(bf16[512,1536]{1,0:T(8,128)(2,1)} %all-gather.4.cloned.1.call-done) | copy-start | bytes 4718596
  241.7 69.3 %all-gather.8.cloned.1.call-start = ((), (), s32[]{:S(2)}) async-start(), calls=%async_computation.4 | async-start | bytes 3538944 | tf_op jit(solution)/shard_map/all_gather | solution.py:44
  278.6 210.7 %reduce-scatter.5.cloned.1.call-start = ((), (), s32[]{:S(2)}) async-start(), calls=%async_computation.5 | async-start | bytes 11796480 | tf_op jit(solution)/shard_map/reduce_scatter | solution.py:48
  320.6 1.7 copy-start
  324.7 164.6 %copy-start.1 = (bf16[1536,768]{0,1:T(8,128)(2,1)S(1)}, bf16[1536,768]{0,1:T(8,128)(2,1)}, u32[]{:S(2)}) copy-start(bf16[1536,768]{0,1:T(8,128)(2,1)} %copy.11) | copy-start | bytes 7077892
  495.1 4.4 copy-start.2
Sparse Core Ops, SparseCore 0:
  9.8 40.7 all-gather.3
  52.4 178.2 all-gather.5
  241.8 33.9 reduce-scatter.6
  278.7 32.2 all-gather.7
  320.7 168.4 reduce-scatter.4
where the time goes:
time: 510 us; the launch traced here: 508 us
  waiting for transfers between devices  450 us (88%)
  local copies, waits for them, and re-layouts  19.4 us (4%)
  matrix products  17.7 us (3%)
  between operations  13.8 us (3%)
  other arithmetic  7.4 us (1%)
    all_gather x1, waiting for transfers between devices, shards(): lax.all_gather(weight, 'col', axis=1, tiled=True)  180 us
    reduce_scatter x1, waiting for transfers between devices, shards(): lax.psum_scatter(grad_panel.astype(jnp.bfloat16), 'col', scatter_dimensio...  160 us
    all_gather x1, waiting for transfers between devices, shards(): gathered = lax.all_gather(tokens, 'row', axis=0, tiled=True)  41.9 us
    unnamed x6, waiting for transfers between devices  35.5 us
    all_gather x1, waiting for transfers between devices, shards(): act_grad = lax.all_gather(local_grad, 'depth', axis=1, tiled=True)  32.4 us
    unnamed x16, local copies, waits for them, and re-layouts  19.4 us
  transfers between devices with their start and end apart: 5, of which 5 were waited for; matrix products, arithmetic and copies ran while one was open for 1% of the time, Pallas kernels for 0%

commit v1 on v0

v1 whole, which is shorter than its diff:
```python
import jax
import jax.numpy as jnp
from jax import lax
from jax.sharding import PartitionSpec as P

D = 12288


gelu_coef = 0.7978845608028654
cubic_coef = 0.044715
lion_rate = 0.5
decay_rate = 0.1
beta_one = 0.9
beta_two = 0.99
smooth_tau = 0.1


def gelu_pair(preact):
    tangent = jnp.tanh(gelu_coef * (preact + cubic_coef * preact * preact * preact))
    gelu_value = 0.5 * preact * (1.0 + tangent)
    gelu_slope = 0.5 * (1.0 + tangent) + 0.5 * preact * (1.0 - tangent * tangent) * gelu_coef * (
        1.0 + 3.0 * cubic_coef * preact * preact
    )
    return (gelu_value, gelu_slope)


def shards(tokens, weight, moment, upstream):
    rows = lax.axis_size("row")
    cols = lax.axis_size("col")
    depth = lax.axis_size("depth")
    tok = tokens.shape[0]
    half = upstream.shape[2]
    cores = depth // cols
    fan_scale = D ** (-0.5)
    there = [
        (c * depth + x * cores + b, x * depth + c * cores + b)
        for c in range(cols)
        for x in range(cols)
        for b in range(cores)
    ]
    back = [(to, fro) for fro, to in there]
    up = lax.ppermute(upstream, ("col", "depth"), there)
    gathered = lax.all_gather(tokens, ("row", "col"), axis=0, tiled=True)
    partial_value = jnp.dot(gathered, weight, preferred_element_type=jnp.float32).astype(jnp.bfloat16)
    blocks = partial_value.reshape(rows, cols, tok, cores, half).transpose(1, 3, 0, 2, 4)
    summed = lax.psum_scatter(
        blocks.reshape(depth * rows * tok, half), "depth", scatter_dimension=0, tiled=True
    ).astype(jnp.float32)
    gelu_value, gelu_slope = gelu_pair(summed * fan_scale)
    activated = gelu_value.astype(jnp.bfloat16).reshape(upstream.shape)
    activated = lax.ppermute(activated, ("col", "depth"), back)
    local_grad = (up.reshape(rows * tok, half).astype(jnp.float32) * gelu_slope).astype(jnp.bfloat16)
    act_grad = lax.all_gather(local_grad, "depth", axis=0, tiled=True)
    act_grad = act_grad.reshape(cols, cores, rows, tok, half).transpose(2, 0, 3, 1, 4)
    act_grad = act_grad.reshape(rows * cols * tok, cores * half)
    grad_full = fan_scale * lax.dot_general(
        gathered, act_grad, (((0,), (0,)), ((), ())), preferred_element_type=jnp.float32
    )
    moment_f = moment.astype(jnp.float32)
    weight_f = weight.astype(jnp.float32)
    blended = beta_one * moment_f + (1.0 - beta_one) * grad_full
    update = blended / jnp.sqrt(blended * blended + smooth_tau * smooth_tau)
    new_weight = (weight_f - lion_rate * (update + decay_rate * weight_f)).astype(jnp.bfloat16)
    new_moment = (beta_two * moment_f + (1.0 - beta_two) * grad_full).astype(jnp.bfloat16)
    return (activated, new_weight, new_moment)


def solution(mesh):
    placed = (
        P(("row", "col"), "depth"),
        P("depth", ("row", "col")),
        P("depth", ("row", "col")),
        P(None, "col", ("row", "depth")),
    )
    return jax.shard_map(
        shards,
        mesh=mesh,
        in_specs=placed,
        out_specs=(
            P(None, "col", ("row", "depth")),
            P("depth", ("row", "col")),
            P("depth", ("row", "col")),
        ),
        check_vma=False,
    )
```

time: 510 us -> 343 us (0.67)
  waiting for transfers between devices: 450 us -> 273 us
  local copies, waits for them, and re-layouts: 19.4 us -> 27.9 us
    reduce_scatter x1, waiting for transfers between devices: 160 us -> 42.6 us  [shards(): lax.psum_scatter(blocks.reshape(depth * rows * tok, half), 'depth', scatt...]
    unnamed x6 -> x3, waiting for transfers between devices: 35.5 us -> 0.71 us
    all_gather x3 -> x2, waiting for transfers between devices: 254 us -> 229 us  [the longest x1 197 us: shards(): gathered = lax.all_gather(tokens, ('row', 'col'), axis=0, tiled=True)]
    reshape x0 -> x3, local copies, waits for them, and re-layouts: none -> 13.4 us  [the longest x2 8.24 us: shards(): partial_value.reshape(rows, cols, tok, cores, half).transpose(1, 3, 0, 2, 4)]
    unnamed x16 -> x14, local copies, waits for them, and re-layouts: 19.4 us -> 14.5 us
  transfers between devices with their start and end apart: 5 -> 5, of which waited for: 5 -> 3; matrix products, arithmetic and copies ran while one was open for 1% -> 2% of each run, Pallas kernels for 0% -> 0%
where the time goes in v1:
time: 343 us; the launch traced here: 340 us
  waiting for transfers between devices  273 us (80%)
  local copies, waits for them, and re-layouts  27.9 us (8%)
  matrix products  21 us (6%)
  between operations  13.8 us (4%)
    all_gather x1, waiting for transfers between devices, shards(): gathered = lax.all_gather(tokens, ('row', 'col'), axis=0, tiled=True)  197 us
    reduce_scatter x1, waiting for transfers between devices, shards(): lax.psum_scatter(blocks.reshape(depth * rows * tok, half), 'depth', scatt...  42.6 us
    all_gather x1, waiting for transfers between devices, shards(): act_grad = lax.all_gather(local_grad, 'depth', axis=0, tiled=True)  32.8 us
    unnamed x14, local copies, waits for them, and re-layouts  14.5 us
    dot_general x1, matrix products, shards(): lax.dot_general(gathered, act_grad, (((0,), (0,)), ((), ())), preferred_e...  11.9 us
    dot_general x1, matrix products, shards(): jnp.dot(gathered, weight, preferred_element_type=jnp.float32)  9.08 us
    reshape x2, local copies, waits for them, and re-layouts, shards(): partial_value.reshape(rows, cols, tok, cores, half).transpose(1, 3, 0, 2, 4)  8.24 us
  transfers between devices with their start and end apart: 5, of which 3 were waited for; matrix products, arithmetic and copies ran while one was open for 2% of the time, Pallas kernels for 0%

profile of v1, /device:TPU:1, one launch (start us, length us, event | category | flops | bytes accessed | tf_op | source)
XLA Modules:
  0.0 339.6 jit_solution(10911719882781538456)
XLA Ops:
  7.2 0.0 all-gather.3.cloned.1.call-start
  7.2 0.7 all-gather.3.cloned.1.call-update
  7.9 0.0 reduce-scatter.2.cloned.1.call-start
  7.9 196.6 %all-gather.3.cloned.1.call-done = bf16[2048,1536]{1,0:T(8,128)(2,1)} async-done(((bf16[64,1536]{1,0:T(8,128)(2,1)}), bf16[2048,1536]{1,0:T(8,128)(2,1)}) %all-gather.3.cloned.1.call-update) | async-done | bytes 6291472 | tf_op jit(solution)/shard_map/all_gather | solution.py:43
  204.6 9.1 %convolution_convert_fusion = bf16[2048,768]{1,0:T(8,128)(2,1)} fusion(bf16[2048,1536]{1,0:T(8,128)(2,1)} %all-gather.3.cloned.1.call-done, bf16[1536,768]{1,0:T(8,128)(2,1)} %param.5), kind=kOutput, calls=%fused_computation.10 | convolution fusion | flops 4833411072 | bytes 11796480 | tf_op jit(solution)/shard_map/dot_general | solution.py:44
  213.6 5.8 %reshape.24 = bf16[8,4,64,2,384]{4,3,2,1,0:T(2,128)(2,1)S(1)} reshape(bf16[2048,768]{1,0:T(8,128)(2,1)} %convolution_convert_fusion) | data formatting | bytes 6291456 | tf_op jit(solution)/shard_map/reshape | solution.py:45
  219.5 0.0 copy-start.3
  219.5 2.4 copy.11
  221.9 0.0 copy-start
  221.9 0.0 reduce-scatter.2.cloned.1.call-update
  221.9 0.0 all-gather.5.cloned.1.call-start
  222.0 0.0 copy-done.3
  222.0 0.8 collective-permute-start.1
  222.8 0.0 collective-permute-done.1
  222.8 42.6 %reduce-scatter.2.cloned.1.call-done = bf16[512,384]{1,0:T(8,128)(2,1)} async-done(((bf16[4096,384]{1,0:T(8,128)(2,1)}), bf16[512,384]{1,0:T(8,128)(2,1)}) %reduce-scatter.2.cloned.1.call-update) | async-done | bytes 393232 | tf_op jit(solution)/shard_map/reduce_scatter | solution.py:46
  265.4 2.4 fusion.17
  267.8 0.0 all-gather.5.cloned.1.call-update
  267.8 0.9 collective-permute-start
  268.7 0.0 copy-done
  268.7 2.4 copy.12
  271.1 2.8 copy.13
  274.0 0.0 collective-permute-done
  274.0 32.8 %all-gather.5.cloned.1.call-done = bf16[4096,384]{1,0:T(8,128)(2,1)} async-done(((bf16[512,384]{1,0:T(8,128)(2,1)}), bf16[4096,384]{1,0:T(8,128)(2,1)}) %all-gather.5.cloned.1.call-update) | async-done | bytes 3145744 | tf_op jit(solution)/shard_map/all_gather | solution.py:53
  306.8 5.1 %copy.14 = bf16[4,2,8,64,384]{4,1,3,0,2:T(2,128)(2,1)S(1)} copy(bf16[4,2,8,64,384]{4,3,2,1,0:T(8,128)(2,1)} %bitcast.24) | data formatting | bytes 6291456 | tf_op jit(solution)/shard_map/reshape | solution.py:54
  311.9 0.0 copy-start.1
  311.9 0.7 copy.17
  312.6 1.0 copy-done.1
  313.6 11.9 %fusion.5 = (bf16[1536,768]{0,1:T(8,128)(2,1)}, bf16[1536,768]{0,1:T(8,128)(2,1)}) fusion(bf16[1536,768]{0,1:T(8,128)(2,1)S(1)} %copy.13, bf16[1536,768]{0,1:T(8,128)(2,1)S(1)} %copy-done.1, bf16[2048,768]{1,0:T(8,128)(2,1)S(1)} %bitcast.25, bf16[2048,1536]{1,0:T(8,128)(2,1)} %all-gather.3.cloned.1.call-done), kind=kOutput, calls=%fused_computation.9 | convolution fusion | flops 4851892224 | bytes 18874368 | tf_op jit(solution)/shard_map/dot_general | solution.py:56
  325.4 0.0 copy-start.2
  325.5 4.4 %copy.15 = bf16[1536,768]{1,0:T(8,128)(2,1)} copy(bf16[1536,768]{0,1:T(8,128)(2,1)} %get-tuple-element.10) | data formatting | bytes 4718592
  329.9 0.0 copy-done.2
  329.9 2.4 copy.16
  332.3 0.7 copy.19
Async XLA Ops:
  7.2 197.4 %all-gather.3.cloned.1.call-start = ((), (), s32[]{:S(2)}) async-start(), calls=%async_computation.1 | async-start | bytes 6488064 | tf_op jit(solution)/shard_map/all_gather | solution.py:43
  7.9 257.5 %reduce-scatter.2.cloned.1.call-start = ((), (), s32[]{:S(2)}) async-start(), calls=%async_computation.2 | async-start | bytes 3538944 | tf_op jit(solution)/shard_map/reduce_scatter | solution.py:46
  219.5 2.5 copy-start.3
  221.9 46.8 %copy-start = (bf16[1536,768]{1,0:T(8,128)(2,1)S(1)}, bf16[1536,768]{1,0:T(8,128)(2,1)}, u32[]{:S(2)}) copy-start(bf16[1536,768]{1,0:T(8,128)(2,1)} %param.5) | copy-start | bytes 7077892
  221.9 84.8 %all-gather.5.cloned.1.call-start = ((), (), s32[]{:S(2)}) async-start(), calls=%async_computation.3 | async-start | bytes 3538944 | tf_op jit(solution)/shard_map/all_gather | solution.py:53
  222.0 0.8 collective-permute-start.1
  267.8 6.2 %collective-permute-start = (bf16[8,64,384]{2,1,0:T(8,128)(2,1)S(1)}, bf16[8,64,384]{2,1,0:T(8,128)(2,1)S(1)}, u32[]{:S(2)}, u32[]{:S(2)}) collective-permute-start(bf16[8,64,384]{2,1,0:T(8,128)(2,1)S(1)} %bitcast.26), channel_id=1, source_target_pairs={{0,0},{1,1},{8,2},{9,3},{16,4},{17,5},{24,6},{25,7},{2,8},{3,9},{1... | collective-permute-start | bytes 1179656 | tf_op jit(solution)/shard_map/ppermute | solution.py:51
  311.9 1.7 copy-start.1
  325.4 4.4 %copy-start.2 = (bf16[1536,768]{0,1:T(8,128)(2,1)S(1)}, bf16[1536,768]{0,1:T(8,128)(2,1)}, u32[]{:S(2)}) copy-start(bf16[1536,768]{0,1:T(8,128)(2,1)} %get-tuple-element.9) | copy-start | bytes 7077892
Sparse Core Ops, SparseCore 0:
  9.8 194.7 all-gather.2
  222.0 43.3 reduce-scatter.1
  267.9 38.7 all-gather.4

commit v2 on v0

v2 whole, which is shorter than its diff:
```python
import jax
import jax.numpy as jnp
from jax import lax
from jax.experimental import pallas as pl
from jax.experimental.pallas import tpu as pltpu
from jax.sharding import PartitionSpec as P

D = 12288
TOK = 64
KA = 1024
KB = 512
FEAT = 1536
HID = 768
HALF = 384
PIECE = 256
NSEM = 176

gelu_coef = 0.7978845608028654
cubic_coef = 0.044715
lion_rate = 0.5
decay_rate = 0.1
beta_one = 0.9
beta_two = 0.99
smooth_tau = 0.1
fan_scale = D ** (-0.5)

MESH = pl.DeviceIdType.MESH


def gelu_pair(preact):
    tangent = jnp.tanh(gelu_coef * (preact + cubic_coef * preact * preact * preact))
    gelu_value = 0.5 * preact * (1.0 + tangent)
    gelu_slope = 0.5 * (1.0 + tangent) + 0.5 * preact * (1.0 - tangent * tangent) * gelu_coef * (
        1.0 + 3.0 * cubic_coef * preact * preact
    )
    return (gelu_value, gelu_slope)


def kernel(
    tok_hbm, w_hbm, m_hbm, up_hbm,
    act_hbm, nw_hbm, nm_hbm,
    xa, xb, wv, mv, acc, own, give, got, part, share, grads, up1, up2, val2, val1,
    send_sem, recv_sem, load_sem, store_sem, act_sem,
):
    row, col, depth = lax.axis_index("row"), lax.axis_index("col"), lax.axis_index("depth")
    y, zlo = lax.rem(row, 4), row // 4
    z = col * 2 + zlo
    x, core = depth // 2, lax.rem(depth, 2)

    def at(y_, z_, x_, core_):
        return (lax.rem(z_, 2) * 4 + y_, z_ // 2, x_ * 2 + core_)

    def y_to(k):
        return at(lax.rem(y + k, 4), z, x, core)

    def z_to(k):
        return at(y, lax.rem(z + k, 8), x, core)

    def x_to(k):
        return at(y, z, lax.rem(x + k, 4), core)

    def col_to(k):
        return (row, lax.rem(col + k, 4), depth)

    partner = at(y, z, x, 1 - core)
    numbers = {}
    sent = {}

    def copy(name, src, dst, device):
        n = numbers.setdefault(name, len(numbers))
        return pltpu.make_async_remote_copy(
            src_ref=src, dst_ref=dst, send_sem=send_sem.at[n], recv_sem=recv_sem.at[n],
            device_id=device, device_id_type=MESH,
        )

    def send(name, src, dst, device):
        c = copy(name, src, dst, device)
        c.start()
        sent[name] = c

    def arrive(name, dst):
        copy(name, dst, dst, partner).wait_recv()

    mine = pl.ds(pl.multiple_of(core * HALF, 128), HALF)
    theirs = pl.ds(pl.multiple_of((1 - core) * HALF, 128), HALF)
    halves = ((mine, pl.ds(0, HALF)), (theirs, pl.ds(HALF, HALF)))
    loads = [
        pltpu.make_async_copy(tok_hbm.at[:, pl.ds(0, KA)], xa.at[0, pl.ds(0, TOK)], load_sem.at[0]),
        pltpu.make_async_copy(tok_hbm.at[:, pl.ds(KA, KB)], xb.at[0, pl.ds(0, TOK)], load_sem.at[1]),
    ]
    for i, (there, here) in enumerate(halves):
        loads.append(pltpu.make_async_copy(w_hbm.at[:, there], wv.at[:, here], load_sem.at[2 + i]))
    for i, (there, here) in enumerate(halves):
        loads.append(pltpu.make_async_copy(m_hbm.at[:, there], mv.at[:, here], load_sem.at[4 + i]))

    def home_row(x_of, x_home):
        return lax.rem(y + x_of + col + 4 - x_home, 4)

    loads.append(pltpu.make_async_copy(up_hbm.at[:, home_row(x, x)], up1.at[x], load_sem.at[6]))
    for c in loads:
        c.start()

    barrier = pltpu.get_barrier_semaphore()
    others = (
        [y_to(1), y_to(3), z_to(1), z_to(7), partner]
        + [x_to(k) for k in (1, 2, 3)]
        + [col_to(k) for k in (1, 2, 3)]
    )
    for other in others:
        pl.semaphore_signal(barrier, inc=1, device_id=other, device_id_type=MESH)
    pl.semaphore_wait(barrier, len(others))

    LOW, HIGH = pl.ds(0, 32), pl.ds(32, 32)

    def rows(dy, lo=0, n=TOK):
        return pl.ds(dy * TOK + lo, n)

    def a_along_z(k):
        down, up = (k - 1) % 8, (1 - k) % 8
        if k < 4:
            send(("az-", k), xa.at[down, rows(0)], xa.at[k, rows(0)], z_to(7))
            send(("az+", k), xa.at[up, rows(0)], xa.at[8 - k, rows(0)], z_to(1))
        else:
            send(("az-", 4), xa.at[3, LOW], xa.at[4, LOW], z_to(7))
            send(("az+", 4), xa.at[5, HIGH], xa.at[4, HIGH], z_to(1))

    def a_from_z(k):
        if k < 4:
            arrive(("az-", k), xa.at[k, rows(0)])
            arrive(("az+", k), xa.at[8 - k, rows(0)])
        else:
            arrive(("az-", 4), xa.at[4, LOW])
            arrive(("az+", 4), xa.at[4, HIGH])

    def a_along_y(dz):
        send(("ay-", dz), xa.at[dz, rows(0)], xa.at[dz, rows(1)], y_to(3))
        send(("ay+", dz), xa.at[dz, rows(0)], xa.at[dz, rows(3)], y_to(1))

    def a_from_y(dz):
        arrive(("ay-", dz), xa.at[dz, rows(1)])
        arrive(("ay+", dz), xa.at[dz, rows(3)])

    def a_far_y(dz):
        send(("af-", dz), xa.at[dz, rows(1, 0, 32)], xa.at[dz, rows(2, 0, 32)], y_to(3))
        send(("af+", dz), xa.at[dz, rows(3, 32, 32)], xa.at[dz, rows(2, 32, 32)], y_to(1))

    def a_from_far(dz):
        arrive(("af-", dz), xa.at[dz, rows(2, 0, 32)])
        arrive(("af+", dz), xa.at[dz, rows(2, 32, 32)])

    def b_along_y():
        send("by-", xb.at[0, rows(0)], xb.at[0, rows(1)], y_to(3))
        send("by+", xb.at[0, rows(0)], xb.at[0, rows(3)], y_to(1))

    def b_far_y():
        arrive("by-", xb.at[0, rows(1)])
        arrive("by+", xb.at[0, rows(3)])
        send("bf-", xb.at[0, rows(1, 0, 32)], xb.at[0, rows(2, 0, 32)], y_to(3))
        send("bf+", xb.at[0, rows(3, 32, 32)], xb.at[0, rows(2, 32, 32)], y_to(1))

    def b_from_far():
        arrive("bf-", xb.at[0, rows(2, 0, 32)])
        arrive("bf+", xb.at[0, rows(2, 32, 32)])

    def b_along_z(k):
        down, up = (k - 1) % 8, (1 - k) % 8
        if k < 4:
            send(("bz-", k), xb.at[down], xb.at[k], z_to(7))
            send(("bz+", k), xb.at[up], xb.at[8 - k], z_to(1))
        else:
            send(("bz-", 4), xb.at[3, pl.ds(0, 128)], xb.at[4, pl.ds(0, 128)], z_to(7))
            send(("bz+", 4), xb.at[5, pl.ds(128, 128)], xb.at[4, pl.ds(128, 128)], z_to(1))

    def b_from_z(k):
        if k < 4:
            arrive(("bz-", k), xb.at[k])
            arrive(("bz+", k), xb.at[8 - k])
        else:
            arrive(("bz-", 4), xb.at[4, pl.ds(0, 128)])
            arrive(("bz+", 4), xb.at[4, pl.ds(128, 128)])

    def up_along_x():
        for k in (1, 2, 3):
            there = lax.rem(x + k, 4)
            send(("ux", k), up_hbm.at[:, home_row(there, x)], up1.at[x], x_to(k))

    def up_along_z():
        loads[6].wait()
        for k in (1, 2, 3):
            arrive(("ux", k), up1.at[lax.rem(x + 4 - k, 4)])
        for k in (1, 2, 3):
            send(("uz", k), up1.at[lax.rem(col + k, 4)], up2.at[4 - k], col_to(k))
        pltpu.make_async_copy(up1.at[col], up2.at[0], load_sem.at[7]).start()

    def up_from_z():
        pltpu.make_async_copy(up1.at[col], up2.at[0], load_sem.at[7]).wait()
        for k in (1, 2, 3):
            arrive(("uz", k), up2.at[4 - k])

    def act_along_z(delta):
        if delta == 0:
            c = pltpu.make_async_copy(val2.at[0], val1.at[col], act_sem.at[0])
            c.start()
            sent["act0"] = None
        else:
            send(("vz", delta), val2.at[delta], val1.at[col], col_to(delta))

    def act_along_x():
        pltpu.make_async_copy(val2.at[0], val1.at[col], act_sem.at[0]).wait()
        for delta in (1, 3, 2):
            arrive(("vz", delta), val1.at[lax.rem(col + 4 - delta, 4)])
        for k in (1, 2, 3):
            there = lax.rem(x + k, 4)
            send(("vx", k), val1.at[there], act_hbm.at[:, home_row(x, there)], x_to(k))
        pltpu.make_async_copy(val1.at[x], act_hbm.at[:, home_row(x, x)], act_sem.at[1]).start()

    def act_done():
        pltpu.make_async_copy(val1.at[x], act_hbm.at[:, home_row(x, x)], act_sem.at[1]).wait()
        for k in (1, 2, 3):
            arrive(("vx", k), act_hbm.at[:, home_row(lax.rem(x + 4 - k, 4), x)])

    def delta_of(dz):
        return lax.rem((zlo + dz) // 2, 4)

    def chunk_rows(dz, x_of):
        dy = lax.rem(x_of + delta_of(dz), 4)
        return pl.ds(pl.multiple_of(dy * TOK, TOK), TOK)

    def forward(dz):
        for n in range(3):
            columns = pl.ds(n * 256, 256)
            value = jnp.dot(xa[dz], wv[pl.ds(0, KA), columns], preferred_element_type=jnp.float32)
            value = value + jnp.dot(xb[dz], wv[pl.ds(KA, KB), columns], preferred_element_type=jnp.float32)
            if n == 0:
                own[dz, :, pl.ds(0, 256)] = value
            elif n == 1:
                own[dz, :, pl.ds(256, 128)] = value[:, :128]
                give[dz, :, pl.ds(0, 128)] = value[:, 128:].astype(jnp.bfloat16)
            else:
                give[dz, :, pl.ds(128, 256)] = value.astype(jnp.bfloat16)
        send(("pair", dz), give.at[dz], got.at[dz], partner)

    def scatter(dz):
        arrive(("pair", dz), got.at[dz])
        total = own[dz] + got[dz].astype(jnp.float32)
        own[dz] = total
        part[dz] = total.astype(jnp.bfloat16)
        for k in (1, 2, 3):
            chunk = chunk_rows(dz, lax.rem(x + k, 4))
            send(("sum", dz, k), part.at[dz, chunk], share.at[dz, k - 1], x_to(k))

    def middle(dz):
        for k in (1, 2, 3):
            arrive(("sum", dz, k), share.at[dz, k - 1])
        chunk = chunk_rows(dz, x)
        summed = own[dz, chunk, :]
        for k in range(3):
            summed = summed + share[dz, k].astype(jnp.float32)
        gelu_value, gelu_slope = gelu_pair(summed * fan_scale)
        delta, odd = delta_of(dz), lax.rem(zlo + dz, 2)
        val2[delta, odd] = gelu_value.astype(jnp.bfloat16)
        grads[dz, 0, chunk, :] = (up2[delta, odd].astype(jnp.float32) * gelu_slope).astype(jnp.bfloat16)
        for k in (1, 2, 3):
            send(("grad", dz, k), grads.at[dz, 0, chunk], grads.at[dz, 0, chunk], x_to(k))

    def pass_on(dz):
        for k in (1, 2, 3):
            arrive(("grad", dz, k), grads.at[dz, 0, chunk_rows(dz, lax.rem(x + 4 - k, 4))])
        send(("both", dz), grads.at[dz, 0], grads.at[dz, 1], partner)

    def gradient_tile(dz, tile):
        both = jnp.concatenate([grads[dz, 0], grads[dz, 1]], axis=1)
        if isinstance(tile, tuple):
            source, columns = tile
        return lax.dot_general(
            source[dz, :, columns], both, (((0,), (0,)), ((), ())), preferred_element_type=jnp.float32
        )

    TILE = 256

    def backward(dz, first=False):
        arrive(("both", dz), grads.at[dz, 1])
        for source, base, count in ((xa, 0, KA // TILE), (xb, KA, KB // TILE)):
            @pl.loop(0, count)
            def _(t):
                columns = pl.ds(pl.multiple_of(t * TILE, TILE), TILE)
                out = pl.ds(pl.multiple_of(base + t * TILE, TILE), TILE)
                value = gradient_tile(dz, (source, columns))
                acc[out, :] = value if first else acc[out, :] + value

    def stores(tile):
        out = pl.ds(pl.multiple_of(tile * TILE, TILE), TILE)
        result = []
        for i, (there, here) in enumerate(halves):
            result.append(pltpu.make_async_copy(wv.at[out, here], nw_hbm.at[out, there], store_sem.at[tile, i]))
            result.append(pltpu.make_async_copy(mv.at[out, here], nm_hbm.at[out, there], store_sem.at[tile, 2 + i]))
        return result

    def finish(dz):
        arrive(("both", dz), grads.at[dz, 1])
        for c in loads[4:6]:
            c.wait()
        for source, base, count in ((xa, 0, KA // TILE), (xb, KA, KB // TILE)):
            @pl.loop(0, count)
            def _(t):
                columns = pl.ds(pl.multiple_of(t * TILE, TILE), TILE)
                out = pl.ds(pl.multiple_of(base + t * TILE, TILE), TILE)
                grad_full = fan_scale * (acc[out, :] + gradient_tile(dz, (source, columns)))
                moment_f = mv[out, :].astype(jnp.float32)
                weight_f = wv[out, :].astype(jnp.float32)
                blended = beta_one * moment_f + (1.0 - beta_one) * grad_full
                update = blended * lax.rsqrt(blended * blended + smooth_tau * smooth_tau)
                wv[out, :] = (weight_f - lion_rate * (update + decay_rate * weight_f)).astype(jnp.bfloat16)
                mv[out, :] = (beta_two * moment_f + (1.0 - beta_two) * grad_full).astype(jnp.bfloat16)
                for c in stores(base // TILE + t):
                    c.start()

    loads[0].wait()
    a_along_z(1)
    loads[1].wait()
    b_along_y()
    a_along_y(0)
    up_along_x()
    b_far_y()
    a_from_z(1)
    a_along_z(2)
    a_along_y(1)
    a_along_y(7)
    b_from_far()
    b_along_z(1)
    up_along_z()
    a_from_y(0)
    a_far_y(0)
    a_from_z(2)
    a_along_z(3)
    a_along_y(2)
    a_along_y(6)
    a_from_far(0)
    for c in loads[2:4]:
        c.wait()
    forward(0)
    for dz in (1, 7):
        a_from_y(dz)
        a_far_y(dz)
    b_from_z(1)
    b_along_z(2)
    scatter(0)
    a_from_z(3)
    a_along_z(4)
    a_along_y(3)
    a_along_y(5)
    a_from_far(1)
    forward(1)
    a_from_far(7)
    forward(7)
    up_from_z()
    middle(0)
    scatter(1)
    scatter(7)
    for dz in (2, 6):
        a_from_y(dz)
        a_far_y(dz)
    b_from_z(2)
    b_along_z(3)
    pass_on(0)
    a_from_z(4)
    a_along_y(4)
    middle(1)
    middle(7)
    act_along_z(0)
    a_from_far(2)
    forward(2)
    a_from_far(6)
    forward(6)
    pass_on(1)
    pass_on(7)
    backward(0, True)
    scatter(2)
    scatter(6)
    for dz in (3, 5):
        a_from_y(dz)
        a_far_y(dz)
    b_from_z(3)
    b_along_z(4)
    middle(2)
    middle(6)
    backward(1)
    backward(7)
    a_from_far(3)
    forward(3)
    a_from_far(5)
    forward(5)
    pass_on(2)
    pass_on(6)
    a_from_y(4)
    a_far_y(4)
    scatter(3)
    scatter(5)
    backward(2)
    backward(6)
    middle(3)
    act_along_z(1)
    middle(5)
    act_along_z(3)
    b_from_z(4)
    a_from_far(4)
    forward(4)
    pass_on(3)
    pass_on(5)
    scatter(4)
    backward(3)
    middle(4)
    act_along_z(2)
    backward(5)
    pass_on(4)
    act_along_x()
    finish(4)
    act_done()
    for tile in range(FEAT // TILE):
        for c in stores(tile):
            c.wait()
    for c in sent.values():
        if c is not None:
            c.wait_send()
    assert len(numbers) <= NSEM, len(numbers)


def shards(tokens, weight, moment, upstream):
    bf16, f32 = jnp.bfloat16, jnp.float32
    any_space = pl.BlockSpec(memory_space=pl.ANY)
    act, new_weight, new_moment = pl.pallas_call(
        kernel,
        out_shape=(
            jax.ShapeDtypeStruct((2, 4, TOK, HALF), bf16),
            jax.ShapeDtypeStruct((FEAT, HID), bf16),
            jax.ShapeDtypeStruct((FEAT, HID), bf16),
        ),
        in_specs=[any_space] * 4,
        out_specs=(any_space,) * 3,
        scratch_shapes=[
            pltpu.VMEM((8, PIECE, KA), bf16),
            pltpu.VMEM((8, PIECE, KB), bf16),
            pltpu.VMEM((FEAT, HID), bf16),
            pltpu.VMEM((FEAT, HID), bf16),
            pltpu.VMEM((FEAT, HID), f32),
            pltpu.VMEM((8, PIECE, HALF), f32),
            pltpu.VMEM((8, PIECE, HALF), bf16),
            pltpu.VMEM((8, PIECE, HALF), bf16),
            pltpu.VMEM((8, PIECE, HALF), bf16),
            pltpu.VMEM((8, 3, TOK, HALF), bf16),
            pltpu.VMEM((8, 2, PIECE, HALF), bf16),
            pltpu.VMEM((4, 2, TOK, HALF), bf16),
            pltpu.VMEM((4, 2, TOK, HALF), bf16),
            pltpu.VMEM((4, 2, TOK, HALF), bf16),
            pltpu.VMEM((4, 2, TOK, HALF), bf16),
            pltpu.SemaphoreType.DMA((NSEM,)),
            pltpu.SemaphoreType.DMA((NSEM,)),
            pltpu.SemaphoreType.DMA((8,)),
            pltpu.SemaphoreType.DMA((FEAT // 256, 4)),
            pltpu.SemaphoreType.DMA((2,)),
        ],
        compiler_params=pltpu.CompilerParams(
            collective_id=0, has_side_effects=True, vmem_limit_bytes=56 * 1024 * 1024
        ),
        cost_estimate=pl.CostEstimate(
            flops=4 * 2048 * FEAT * HID, bytes_accessed=12 * 1024 * 1024, transcendentals=2 * FEAT * HID
        ),
    )(tokens, weight, moment, upstream.reshape(2, 4, TOK, HALF))
    return (act.reshape(upstream.shape), new_weight, new_moment)


def solution(mesh):
    placed = (
        P(("row", "col"), "depth"),
        P("depth", ("row", "col")),
        P("depth", ("row", "col")),
        P(None, "col", ("row", "depth")),
    )
    return jax.shard_map(
        shards,
        mesh=mesh,
        in_specs=placed,
        out_specs=(
            P(None, "col", ("row", "depth")),
            P("depth", ("row", "col")),
            P("depth", ("row", "col")),
        ),
        check_vma=False,
    )
```

time: 510 us -> 109 us (0.21)
  waiting for transfers between devices: 450 us -> 0 us
  Pallas kernels: 0 us -> 101 us
  matrix products: 17.7 us -> 0 us
  between operations: 13.8 us -> 0.64 us
  local copies, waits for them, and re-layouts: 19.4 us -> 6.56 us
  other arithmetic: 7.4 us -> 0 us
    all_gather x3 -> x0, waiting for transfers between devices: 254 us -> none  [the longest x1 180 us: shards(): lax.all_gather(weight, 'col', axis=1, tiled=True)]
    reduce_scatter x1 -> x0, waiting for transfers between devices: 160 us -> none  [shards(): lax.psum_scatter(grad_panel.astype(jnp.bfloat16), 'col', scatter_dimensio...]
    pallas_call x0 -> x1, Pallas kernels: none -> 101 us  [shards(): pl.pallas_call(kernel, out_shape=(jax.ShapeDtypeStruct((2, 4, TOK, HALF),...]
    unnamed x6 -> x0, waiting for transfers between devices: 35.5 us -> none
    dot_general x2 -> x0, matrix products: 17.7 us -> none  [the longest x1 9.59 us: shards(): lax.dot_general(gathered, act_grad, (((0,), (0,)), ((), ())), preferred_e...]
    unnamed x16 -> x5, local copies, waits for them, and re-layouts: 19.4 us -> 6.56 us
    convert_element_type x2 -> x0, other arithmetic: 7.4 us -> none  [the longest x1 5.85 us: shards(): (beta_two * moment_f + (1.0 - beta_two) * grad_full).astype(jnp.bfloat16)]
  transfers between devices with their start and end apart: 5 -> 0, of which waited for: 5 -> 0; matrix products, arithmetic and copies ran while one was open for 1% -> 0% of each run, Pallas kernels for 0% -> 0%
where the time goes in v2:
time: 109 us; the launch traced here: 108 us
  Pallas kernels  101 us (93%)
  local copies, waits for them, and re-layouts  6.56 us (6%)
    pallas_call x1, Pallas kernels, shards(): pl.pallas_call(kernel, out_shape=(jax.ShapeDtypeStruct((2, 4, TOK, HALF),...  101 us
    unnamed x5, local copies, waits for them, and re-layouts  6.56 us

profile of v2, /device:TPU:1, one launch (start us, length us, event | category | flops | bytes accessed | tf_op | source)
XLA Modules:
  0.0 108.0 jit_solution(9642369191825979922)
XLA Ops:
  0.6 100.8 %shard_map.67 = (bf16[2,4,64,384]{3,2,1,0:T(8,128)(2,1)}, bf16[1536,768]{1,0:T(8,128)(2,1)}, bf16[1536,768]{1,0:T(8,128)(2,1)}) custom-call(bf16[64,1536]{1,0:T(8,128)(2,1)} %tok_hbm.1, bf16[1536,768]{1,0:T(8,128)(2,1)} %w_hbm.1, bf16[1536,768]{1,0:T(8,128)(2,1)} %m_hbm.1, bf16[2,4,64,384]{3,2,1,0:T(8,128)(2,1)} %bitcast.3), custom_call_target="tpu_custom_call" | custom-call | flops 9663676416 | bytes 12582912 | tf_op jit(solution)/shard_map/pallas_call | solution.py:431
  101.4 1.8 %copy.10 = bf16[8,64,384]{2,1,0:T(8,128)(2,1)} copy(bf16[8,64,384]{2,1,0:T(8,128)(2,1)} %bitcast.2) | data formatting | bytes 786432
  103.2 0.0 copy-start
  103.2 3.4 %copy.11 = bf16[1536,768]{1,0:T(8,128)(2,1)} copy(bf16[1536,768]{1,0:T(8,128)(2,1)} %get-tuple-element.13) | data formatting | bytes 4718592
  106.6 0.0 copy-done
  106.6 1.4 %copy.12 = bf16[1536,768]{1,0:T(8,128)(2,1)} copy(bf16[1536,768]{1,0:T(8,128)(2,1)S(1)} %copy-done) | data formatting | bytes 4718592
Async XLA Ops:
  103.2 3.4 %copy-start = (bf16[1536,768]{1,0:T(8,128)(2,1)S(1)}, bf16[1536,768]{1,0:T(8,128)(2,1)}, u32[]{:S(2)}) copy-start(bf16[1536,768]{1,0:T(8,128)(2,1)} %get-tuple-element.14) | copy-start | bytes 7077892

commit v3 on v2

v3 whole, which is shorter than its diff:
```python
import functools

import jax
import jax.numpy as jnp
from jax import lax
from jax.experimental import pallas as pl
from jax.experimental.pallas import tpu as pltpu
from jax.sharding import PartitionSpec as P

D = 12288
TOK = 64
KA = 1024
KB = 512
FEAT = 1536
HID = 768
HALF = 384
PIECE = 256
NSEM = 176
UPDATE = 256

gelu_coef = 0.7978845608028654
cubic_coef = 0.044715
lion_rate = 0.5
decay_rate = 0.1
beta_one = 0.9
beta_two = 0.99
smooth_tau = 0.1
fan_scale = D ** (-0.5)

MESH = pl.DeviceIdType.MESH

ORDER = (
    "start", "bfar", "bz10", "az2", "ay1", "af0", "ay7", "u0", "bz11", "bz20", "af1", "az3", "ay2", "uz1", "f0", "s0",
    "bz21", "af7", "ay6", "f1", "bz30", "s1", "af2", "m0", "az4", "ay3", "f7", "s7", "af6", "ay5", "m1", "p0", "bz31",
    "f2", "af3", "b0", "f6", "m7", "p1", "s2", "vz0", "s6", "af5", "ay4", "uz2", "b1", "bz4", "f3", "p7", "f5", "m2",
    "s3", "b7", "af4", "s5", "m6", "p2", "f4", "b2", "s4", "m3", "vz1", "m5", "vz3", "vz2", "p6", "b6", "m4", "vz4",
    "p3", "b3", "p5", "vx", "p4", "b5", "fin",
)


def gelu_pair(preact):
    tangent = jnp.tanh(gelu_coef * (preact + cubic_coef * preact * preact * preact))
    gelu_value = 0.5 * preact * (1.0 + tangent)
    gelu_slope = 0.5 * (1.0 + tangent) + 0.5 * preact * (1.0 - tangent * tangent) * gelu_coef * (
        1.0 + 3.0 * cubic_coef * preact * preact
    )
    return (gelu_value, gelu_slope)


def kernel(
    tok_hbm, w_hbm, up_hbm,
    act_hbm, grad_hbm, last_tok_hbm, last_grad_hbm,
    xa, xb, wv, acc, own, give, got, part, share, grads, up1, up2, val2, val1,
    send_sem, recv_sem, load_sem, store_sem, act_sem, last_sem,
):
    row, col, depth = lax.axis_index("row"), lax.axis_index("col"), lax.axis_index("depth")
    y, zlo = lax.rem(row, 4), row // 4
    z = col * 2 + zlo
    x, core = depth // 2, lax.rem(depth, 2)

    def at(y_, z_, x_, core_):
        return (lax.rem(z_, 2) * 4 + y_, z_ // 2, x_ * 2 + core_)

    def y_to(k):
        return at(lax.rem(y + k, 4), z, x, core)

    def z_to(k):
        return at(y, lax.rem(z + k, 8), x, core)

    def x_to(k):
        return at(y, z, lax.rem(x + k, 4), core)

    def col_to(k):
        return (row, lax.rem(col + k, 4), depth)

    partner = at(y, z, x, 1 - core)
    numbers = {}
    sent = {}

    def copy(name, src, dst, device):
        n = numbers.setdefault(name, len(numbers))
        return pltpu.make_async_remote_copy(
            src_ref=src, dst_ref=dst, send_sem=send_sem.at[n], recv_sem=recv_sem.at[n],
            device_id=device, device_id_type=MESH,
        )

    def send(name, src, dst, device):
        c = copy(name, src, dst, device)
        c.start()
        sent[name] = c

    def arrive(name, dst):
        copy(name, dst, dst, partner).wait_recv()

    mine = pl.ds(pl.multiple_of(core * HALF, 128), HALF)
    theirs = pl.ds(pl.multiple_of((1 - core) * HALF, 128), HALF)
    halves = ((mine, pl.ds(0, HALF)), (theirs, pl.ds(HALF, HALF)))
    loads = [
        pltpu.make_async_copy(tok_hbm.at[:, pl.ds(0, KA)], xa.at[0, pl.ds(0, TOK)], load_sem.at[0]),
        pltpu.make_async_copy(tok_hbm.at[:, pl.ds(KA, KB)], xb.at[0, pl.ds(0, TOK)], load_sem.at[1]),
    ]
    for i, (there, here) in enumerate(halves):
        loads.append(pltpu.make_async_copy(w_hbm.at[:, there], wv.at[:, here], load_sem.at[2 + i]))

    def home_row(x_of, x_home):
        return lax.rem(y + x_of + col + 4 - x_home, 4)

    loads.append(pltpu.make_async_copy(up_hbm.at[:, home_row(x, x)], up1.at[x], load_sem.at[4]))
    for c in loads:
        c.start()

    barrier = pltpu.get_barrier_semaphore()
    others = (
        [y_to(1), y_to(3), z_to(1), z_to(7), partner]
        + [x_to(k) for k in (1, 2, 3)]
    )
    for other in others:
        pl.semaphore_signal(barrier, inc=1, device_id=other, device_id_type=MESH)
    pl.semaphore_wait(barrier, len(others))

    LOW, HIGH = pl.ds(0, 32), pl.ds(32, 32)

    def rows(dy, lo=0, n=TOK):
        return pl.ds(dy * TOK + lo, n)

    def a_along_z(k):
        down, up = (k - 1) % 8, (1 - k) % 8
        if k < 4:
            send(("az-", k), xa.at[down, rows(0)], xa.at[k, rows(0)], z_to(7))
            send(("az+", k), xa.at[up, rows(0)], xa.at[8 - k, rows(0)], z_to(1))
        else:
            send(("az-", 4), xa.at[3, LOW], xa.at[4, LOW], z_to(7))
            send(("az+", 4), xa.at[5, HIGH], xa.at[4, HIGH], z_to(1))

    def a_from_z(k):
        if k < 4:
            arrive(("az-", k), xa.at[k, rows(0)])
            arrive(("az+", k), xa.at[8 - k, rows(0)])
        else:
            arrive(("az-", 4), xa.at[4, LOW])
            arrive(("az+", 4), xa.at[4, HIGH])

    def a_along_y(dz):
        send(("ay-", dz), xa.at[dz, rows(0)], xa.at[dz, rows(1)], y_to(3))
        send(("ay+", dz), xa.at[dz, rows(0)], xa.at[dz, rows(3)], y_to(1))

    def a_from_y(dz):
        arrive(("ay-", dz), xa.at[dz, rows(1)])
        arrive(("ay+", dz), xa.at[dz, rows(3)])

    def a_far_y(dz):
        send(("af-", dz), xa.at[dz, rows(1, 0, 32)], xa.at[dz, rows(2, 0, 32)], y_to(3))
        send(("af+", dz), xa.at[dz, rows(3, 32, 32)], xa.at[dz, rows(2, 32, 32)], y_to(1))

    def a_from_far(dz):
        arrive(("af-", dz), xa.at[dz, rows(2, 0, 32)])
        arrive(("af+", dz), xa.at[dz, rows(2, 32, 32)])

    def b_along_y():
        send("by-", xb.at[0, rows(0)], xb.at[0, rows(1)], y_to(3))
        send("by+", xb.at[0, rows(0)], xb.at[0, rows(3)], y_to(1))

    def b_from_y():
        arrive("by-", xb.at[0, rows(1)])
        arrive("by+", xb.at[0, rows(3)])

    def b_far_y():
        send("bf-", xb.at[0, rows(1, 0, 32)], xb.at[0, rows(2, 0, 32)], y_to(3))
        send("bf+", xb.at[0, rows(3, 32, 32)], xb.at[0, rows(2, 32, 32)], y_to(1))

    def b_from_far():
        arrive("bf-", xb.at[0, rows(2, 0, 32)])
        arrive("bf+", xb.at[0, rows(2, 32, 32)])

    HALVES = (pl.ds(0, 128), pl.ds(128, 128))

    def b_along_z(k, h):
        down, up, part_rows = (k - 1) % 8, (1 - k) % 8, HALVES[h]
        send(("bz-", k, h), xb.at[down, part_rows], xb.at[k, part_rows], z_to(7))
        send(("bz+", k, h), xb.at[up, part_rows], xb.at[8 - k, part_rows], z_to(1))

    def b_from_z(k, h):
        arrive(("bz-", k, h), xb.at[k, HALVES[h]])
        arrive(("bz+", k, h), xb.at[8 - k, HALVES[h]])

    def b_far_z():
        send("bq-", xb.at[3, HALVES[0]], xb.at[4, HALVES[0]], z_to(7))
        send("bq+", xb.at[5, HALVES[1]], xb.at[4, HALVES[1]], z_to(1))

    def b_from_far_z():
        arrive("bq-", xb.at[4, HALVES[0]])
        arrive("bq+", xb.at[4, HALVES[1]])

    def up_along_x():
        for k in (1, 2, 3):
            there = lax.rem(x + k, 4)
            send(("ux", k), up_hbm.at[:, home_row(there, x)], up1.at[x], x_to(k))

    def up_from_x():
        loads[4].wait()
        for k in (1, 2, 3):
            arrive(("ux", k), up1.at[lax.rem(x + 4 - k, 4)])

    stay = pltpu.make_async_copy(up1.at[col], up2.at[0], load_sem.at[5])

    def up_along_z(ks):
        for k in ks:
            send(("uz", k), up1.at[lax.rem(col + k, 4)], up2.at[4 - k], col_to(k))

    def up_from_z(ks):
        for k in ks:
            arrive(("uz", k), up2.at[4 - k])

    def act_along_z(delta):
        if delta == 0:
            pltpu.make_async_copy(val2.at[0], val1.at[col], act_sem.at[0]).start()
        else:
            send(("vz", delta), val2.at[delta], val1.at[col], col_to(delta))

    def act_half_along_z(odd, name):
        send((name, 2), val2.at[2, odd], val1.at[col, odd], col_to(2))

    def act_from_z(delta):
        arrive(("vz", delta), val1.at[lax.rem(col + 4 - delta, 4)])

    def act_half_from_z(odd, name):
        arrive((name, 2), val1.at[lax.rem(col + 2, 4), odd])

    def act_along_x():
        pltpu.make_async_copy(val2.at[0], val1.at[col], act_sem.at[0]).wait()
        for k in (1, 2, 3):
            there = lax.rem(x + k, 4)
            send(("vx", k), val1.at[there], act_hbm.at[:, home_row(x, there)], x_to(k))
        pltpu.make_async_copy(val1.at[x], act_hbm.at[:, home_row(x, x)], act_sem.at[1]).start()

    def act_done():
        pltpu.make_async_copy(val1.at[x], act_hbm.at[:, home_row(x, x)], act_sem.at[1]).wait()
        for k in (1, 2, 3):
            arrive(("vx", k), act_hbm.at[:, home_row(lax.rem(x + 4 - k, 4), x)])

    def delta_of(dz):
        return lax.rem((zlo + dz) // 2, 4)

    def chunk_rows(dz, x_of):
        dy = lax.rem(x_of + delta_of(dz), 4)
        return pl.ds(pl.multiple_of(dy * TOK, TOK), TOK)

    def forward(dz):
        for n in range(3):
            columns = pl.ds(n * 256, 256)
            value = jnp.dot(xa[dz], wv[pl.ds(0, KA), columns], preferred_element_type=jnp.float32)
            value = value + jnp.dot(xb[dz], wv[pl.ds(KA, KB), columns], preferred_element_type=jnp.float32)
            if n == 0:
                own[dz, :, pl.ds(0, 256)] = value
            elif n == 1:
                own[dz, :, pl.ds(256, 128)] = value[:, :128]
                give[dz, :, pl.ds(0, 128)] = value[:, 128:].astype(jnp.bfloat16)
            else:
                give[dz, :, pl.ds(128, 256)] = value.astype(jnp.bfloat16)
        send(("pair", dz), give.at[dz], got.at[dz], partner)

    def scatter(dz):
        total = own[dz] + got[dz].astype(jnp.float32)
        own[dz] = total
        part[dz] = total.astype(jnp.bfloat16)
        for k in (1, 2, 3):
            chunk = chunk_rows(dz, lax.rem(x + k, 4))
            send(("sum", dz, k), part.at[dz, chunk], share.at[dz, k - 1], x_to(k))

    def middle(dz):
        chunk = chunk_rows(dz, x)
        summed = own[dz, chunk, :]
        for k in range(3):
            summed = summed + share[dz, k].astype(jnp.float32)
        gelu_value, gelu_slope = gelu_pair(summed * fan_scale)
        delta, odd = delta_of(dz), lax.rem(zlo + dz, 2)
        val2[delta, odd] = gelu_value.astype(jnp.bfloat16)
        grads[dz, 0, chunk, :] = (up2[delta, odd].astype(jnp.float32) * gelu_slope).astype(jnp.bfloat16)
        for k in (1, 2, 3):
            send(("grad", dz, k), grads.at[dz, 0, chunk], grads.at[dz, 0, chunk], x_to(k))

    def pass_on(dz):
        send(("both", dz), grads.at[dz, 0], grads.at[dz, 1], partner)

    def gradient_tile(dz, tile):
        both = jnp.concatenate([grads[dz, 0], grads[dz, 1]], axis=1)
        if isinstance(tile, tuple):
            source, columns = tile
        return lax.dot_general(
            source[dz, :, columns], both, (((0,), (0,)), ((), ())), preferred_element_type=jnp.float32
        )

    TILE = 256
    begun = []

    def backward(dz):
        first = not begun
        begun.append(dz)
        last = len(begun) == 7

        for source, base, count in ((xa, 0, KA // TILE), (xb, KA, KB // TILE)):
            @pl.loop(0, count)
            def _(t):
                columns = pl.ds(pl.multiple_of(t * TILE, TILE), TILE)
                out = pl.ds(pl.multiple_of(base + t * TILE, TILE), TILE)
                value = gradient_tile(dz, (source, columns))
                acc[out, :] = value if first else acc[out, :] + value
                if last:
                    for c in stores(base // TILE + t):
                        c.start()

    def stores(tile):
        out = pl.ds(pl.multiple_of(tile * TILE, TILE), TILE)
        result = []
        for i, (there, here) in enumerate(halves):
            result.append(pltpu.make_async_copy(acc.at[out, here], grad_hbm.at[out, there], store_sem.at[tile, i]))
        return result

    last_tok = [
        pltpu.make_async_copy(xa.at[4], last_tok_hbm.at[:, pl.ds(0, KA)], last_sem.at[0]),
        pltpu.make_async_copy(xb.at[4], last_tok_hbm.at[:, pl.ds(KA, KB)], last_sem.at[1]),
    ]
    last_grad = [
        pltpu.make_async_copy(grads.at[4, 0], last_grad_hbm.at[:, mine], last_sem.at[2]),
        pltpu.make_async_copy(grads.at[4, 1], last_grad_hbm.at[:, theirs], last_sem.at[3]),
    ]

    def forward_last():
        forward(4)
        for c in last_tok:
            c.start()

    def finish():
        for c in last_grad:
            c.start()

    def sums_from(dz):
        for k in (1, 2, 3):
            arrive(("sum", dz, k), share.at[dz, k - 1])

    def grads_from(dz):
        for k in (1, 2, 3):
            arrive(("grad", dz, k), grads.at[dz, 0, chunk_rows(dz, lax.rem(x + 4 - k, 4))])

    def wait_all(copies):
        for c in copies:
            c.wait()

    received = {
        "tok_a": loads[0].wait, "tok_b": loads[1].wait, "by": b_from_y, "bf": b_from_far, "bz4": b_from_far_z,
        "ux": up_from_x, "uz0": stay.wait, "uz1": lambda: up_from_z((1, 3)), "uz2": lambda: up_from_z((2,)),
        "w": lambda: wait_all(loads[2:4]),
    }
    for k in (1, 2, 3, 4):
        received[f"az{k}"] = functools.partial(a_from_z, k)
        for h in (0, 1):
            received[f"bz{k}{h}"] = functools.partial(b_from_z, k, h)
    for dz in range(8):
        received[f"ay{dz}"] = functools.partial(a_from_y, dz)
        received[f"af{dz}"] = functools.partial(a_from_far, dz)
        received[f"pair{dz}"] = functools.partial(lambda d: arrive(("pair", d), got.at[d]), dz)
        received[f"sum{dz}"] = functools.partial(sums_from, dz)
        received[f"grad{dz}"] = functools.partial(grads_from, dz)
        received[f"both{dz}"] = functools.partial(lambda d: arrive(("both", d), grads.at[d, 1]), dz)
    for delta in (1, 2, 3):
        received[f"vz{delta}"] = functools.partial(act_from_z, delta)

    def begin():
        need("tok_a")
        a_along_z(1)
        need("tok_b")
        b_along_y()
        a_along_y(0)
        up_along_x()

    events = {
        "start": ((), begin),
        "bfar": (("by",), b_far_y),
        "bz4": (("bz30", "bz31"), b_far_z),
        "u0": (("ux",), stay.start),
        "uz1": (("ux", "az2"), lambda: up_along_z((1, 3))),
        "uz2": (("ux", "az4"), lambda: up_along_z((2,))),
        "vx": (("vz1", "vz2", "vz3", "vz4"), act_along_x),
        "fin": (("both4",), finish),
    }
    for k in (2, 3, 4):
        events[f"az{k}"] = ((f"az{k - 1}",), functools.partial(a_along_z, k))
    for h in (0, 1):
        events[f"bz1{h}"] = (("by", "bf") if h else ("by",), functools.partial(b_along_z, 1, h))
        for k in (2, 3):
            events[f"bz{k}{h}"] = ((f"bz{k - 1}{h}",), functools.partial(b_along_z, k, h))
    for dz in range(8):
        k = min(dz, 8 - dz)
        lower = {0: ("by", "bf"), 4: ("bz4",)}.get(k, (f"bz{k}0", f"bz{k}1"))
        upper = {0: ("uz0",), 1: ("uz0", "uz1"), 2: ("uz1",), 3: ("uz1", "uz2"), 4: ("uz2",)}[k]
        if dz:
            events[f"ay{dz}"] = ((f"az{k}",), functools.partial(a_along_y, dz))
        events[f"af{dz}"] = ((f"ay{dz}",), functools.partial(a_far_y, dz))
        events[f"f{dz}"] = (("w", f"af{dz}") + lower, functools.partial(forward, dz))
        events[f"s{dz}"] = ((f"pair{dz}",), functools.partial(scatter, dz))
        events[f"m{dz}"] = ((f"sum{dz}",) + upper, functools.partial(middle, dz))
        events[f"p{dz}"] = ((f"grad{dz}",), functools.partial(pass_on, dz))
        events[f"b{dz}"] = ((f"both{dz}",), functools.partial(backward, dz))
    events["f4"] = (events["f4"][0], forward_last)
    for delta in range(4):
        events[f"vz{delta}"] = ((), functools.partial(act_along_z, delta))
    events["vz2"] = ((), functools.partial(act_half_along_z, 1 - zlo, "va"))
    events["vz4"] = ((), functools.partial(act_half_along_z, zlo, "vb"))
    received["vz2"] = functools.partial(act_half_from_z, 1 - zlo, "va")
    received["vz4"] = functools.partial(act_half_from_z, zlo, "vb")

    had = set()

    def need(name):
        if name not in had:
            had.add(name)
            received[name]()

    for name in ORDER:
        needs, do = events[name]
        for other in needs:
            need(other)
        do()
    act_done()
    for tile in range(FEAT // TILE):
        for c in stores(tile):
            c.wait()
    for c in last_tok + last_grad:
        c.wait()
    for c in sent.values():
        c.wait_send()
    assert len(numbers) <= NSEM, len(numbers)


def update(act_in, tok_ref, grad_ref, sum_ref, w_ref, m_ref, act_out, nw_ref, nm_ref, act_sem):
    step = pl.program_id(0)
    act = pltpu.make_async_copy(act_in, act_out, act_sem)

    @pl.when(step == 0)
    def _():
        act.start()

    grad_sum = sum_ref[...] + lax.dot_general(
        tok_ref[...], grad_ref[...], (((0,), (0,)), ((), ())), preferred_element_type=jnp.float32
    )
    moment_f = m_ref[...].astype(jnp.float32)
    weight_f = w_ref[...].astype(jnp.float32)
    blended = beta_one * moment_f + ((1.0 - beta_one) * fan_scale) * grad_sum
    sign = blended * lax.rsqrt(blended * blended + smooth_tau * smooth_tau)
    nw_ref[...] = ((1.0 - lion_rate * decay_rate) * weight_f - lion_rate * sign).astype(jnp.bfloat16)
    nm_ref[...] = (beta_two * moment_f + ((1.0 - beta_two) * fan_scale) * grad_sum).astype(jnp.bfloat16)

    @pl.when(step == pl.num_programs(0) - 1)
    def _():
        act.wait()


def shards(tokens, weight, moment, upstream):
    bf16, f32 = jnp.bfloat16, jnp.float32
    any_space = pl.BlockSpec(memory_space=pl.ANY)
    act_shape = jax.ShapeDtypeStruct((2, 4, TOK, HALF), bf16)
    block_shape = jax.ShapeDtypeStruct((FEAT, HID), bf16)
    act, grad_sum, last_tok, last_grad = pl.pallas_call(
        kernel,
        out_shape=(
            act_shape,
            jax.ShapeDtypeStruct((FEAT, HID), f32),
            jax.ShapeDtypeStruct((PIECE, FEAT), bf16),
            jax.ShapeDtypeStruct((PIECE, HID), bf16),
        ),
        in_specs=[any_space] * 3,
        out_specs=(any_space,) * 4,
        scratch_shapes=[
            pltpu.VMEM((8, PIECE, KA), bf16),
            pltpu.VMEM((8, PIECE, KB), bf16),
            pltpu.VMEM((FEAT, HID), bf16),
            pltpu.VMEM((FEAT, HID), f32),
            pltpu.VMEM((8, PIECE, HALF), f32),
            pltpu.VMEM((8, PIECE, HALF), bf16),
            pltpu.VMEM((8, PIECE, HALF), bf16),
            pltpu.VMEM((8, PIECE, HALF), bf16),
            pltpu.VMEM((8, 3, TOK, HALF), bf16),
            pltpu.VMEM((8, 2, PIECE, HALF), bf16),
            pltpu.VMEM((4, 2, TOK, HALF), bf16),
            pltpu.VMEM((4, 2, TOK, HALF), bf16),
            pltpu.VMEM((4, 2, TOK, HALF), bf16),
            pltpu.VMEM((4, 2, TOK, HALF), bf16),
            pltpu.SemaphoreType.DMA((NSEM,)),
            pltpu.SemaphoreType.DMA((NSEM,)),
            pltpu.SemaphoreType.DMA((6,)),
            pltpu.SemaphoreType.DMA((FEAT // 256, 2)),
            pltpu.SemaphoreType.DMA((2,)),
            pltpu.SemaphoreType.DMA((4,)),
        ],
        compiler_params=pltpu.CompilerParams(
            collective_id=0, has_side_effects=True, vmem_limit_bytes=58 * 1024 * 1024
        ),
        cost_estimate=pl.CostEstimate(
            flops=4 * 2048 * FEAT * HID, bytes_accessed=12 * 1024 * 1024, transcendentals=2 * FEAT * HID
        ),
    )(tokens, weight, upstream.reshape(2, 4, TOK, HALF))
    tile = pl.BlockSpec((UPDATE, HID), lambda t: (t, 0))
    act, new_weight, new_moment = pl.pallas_call(
        update,
        out_shape=(act_shape, block_shape, block_shape),
        grid=(FEAT // UPDATE,),
        in_specs=[
            any_space,
            pl.BlockSpec((PIECE, UPDATE), lambda t: (0, t)),
            pl.BlockSpec((PIECE, HID), lambda t: (0, 0)),
            tile,
            tile,
            tile,
        ],
        out_specs=(any_space, tile, tile),
        scratch_shapes=[pltpu.SemaphoreType.DMA],
        compiler_params=pltpu.CompilerParams(vmem_limit_bytes=24 * 1024 * 1024),
        cost_estimate=pl.CostEstimate(
            flops=2 * PIECE * FEAT * HID, bytes_accessed=16 * FEAT * HID, transcendentals=FEAT * HID
        ),
    )(act, last_tok, last_grad, grad_sum, weight, moment)
    return (act.reshape(upstream.shape), new_weight, new_moment)


def solution(mesh):
    placed = (
        P(("row", "col"), "depth"),
        P("depth", ("row", "col")),
        P("depth", ("row", "col")),
        P(None, "col", ("row", "depth")),
    )
    return jax.shard_map(
        shards,
        mesh=mesh,
        in_specs=placed,
        out_specs=(
            P(None, "col", ("row", "depth")),
            P("depth", ("row", "col")),
            P("depth", ("row", "col")),
        ),
        check_vma=False,
    )
```

time: 109 us -> 90.5 us (0.83)
  Pallas kernels: 101 us -> 84.1 us
  local copies, waits for them, and re-layouts: 6.56 us -> 5.46 us
    pallas_call x1 -> x2, Pallas kernels: 101 us -> 84.1 us  [the longest x1 78.9 us: shards(): pl.pallas_call(kernel, out_shape=(act_shape, jax.ShapeDtypeStruct((FEAT,...]
    unnamed x5 -> x12, local copies, waits for them, and re-layouts: 6.56 us -> 5.46 us
where the time goes in v3:
time: 90.5 us; the launch traced here: 90.2 us
  Pallas kernels  84.1 us (93%)
  local copies, waits for them, and re-layouts  5.46 us (6%)
    pallas_call x1, Pallas kernels, shards(): pl.pallas_call(kernel, out_shape=(act_shape, jax.ShapeDtypeStruct((FEAT,...  78.9 us
    unnamed x12, local copies, waits for them, and re-layouts  5.46 us
    pallas_call x1, Pallas kernels, shards(): pl.pallas_call(update, out_shape=(act_shape, block_shape, block_shape), g...  5.17 us

profile of v3, /device:TPU:1, one launch (start us, length us, event | category | flops | bytes accessed | tf_op | source)
XLA Modules:
  0.0 90.2 jit_solution(6650428282868517849)
XLA Ops:
  0.6 0.0 copy-start.1
  0.6 0.0 copy-start.2
  0.7 78.9 %shard_map.67 = (bf16[2,4,64,384]{3,2,1,0:T(8,128)(2,1)}, f32[1536,768]{1,0:T(8,128)}, bf16[256,1536]{1,0:T(8,128)(2,1)}, bf16[256,768]{1,0:T(8,128)(2,1)}) custom-call(bf16[64,1536]{1,0:T(8,128)(2,1)} %tok_hbm.1, bf16[1536,768]{1,0:T(8,128)(2,1)} %w_ref.1, bf16[2,4,64,384]{3,2,1,0:T(8,128)(2,1)} %bitcast.2), custom_call_target="tpu_custom_call" | custom-call | flops 9663676416 | bytes 12582912 | tf_op jit(solution)/shard_map/pallas_call | solution.py:463
  79.6 0.0 copy-done.1
  79.6 0.0 copy-done.2
  79.6 0.0 copy-start
  79.6 2.3 %copy-done = f32[1536,768]{1,0:T(8,128)S(1)} copy-done((f32[1536,768]{1,0:T(8,128)S(1)}, f32[1536,768]{1,0:T(8,128)}, u32[]{:S(2)}) %copy-start) | copy-done | bytes 4718616
  81.9 0.0 copy-start.3
  81.9 1.1 %copy-done.3 = bf16[256,1536]{1,0:T(8,128)(2,1)S(1)} copy-done((bf16[256,1536]{1,0:T(8,128)(2,1)S(1)}, bf16[256,1536]{1,0:T(8,128)(2,1)}, u32[]{:S(2)}) %copy-start.3) | copy-done | bytes 786456
  83.0 0.0 copy-start.4
  83.1 1.0 %copy-done.4 = bf16[2,4,64,384]{3,2,1,0:T(8,128)(2,1)S(1)} copy-done((bf16[2,4,64,384]{3,2,1,0:T(8,128)(2,1)S(1)}, bf16[2,4,64,384]{3,2,1,0:T(8,128)(2,1)}, u32[]{:S(2)}) %copy-start.4) | copy-done | bytes 393240
  84.0 0.0 copy-start.5
  84.0 1.0 %copy-done.5 = bf16[256,768]{1,0:T(8,128)(2,1)S(1)} copy-done((bf16[256,768]{1,0:T(8,128)(2,1)S(1)}, bf16[256,768]{1,0:T(8,128)(2,1)}, u32[]{:S(2)}) %copy-start.5) | copy-done | bytes 393240
  85.0 5.2 %shard_map.68 = (bf16[2,4,64,384]{3,2,1,0:T(8,128)(2,1)}, bf16[1536,768]{1,0:T(8,128)(2,1)}, bf16[1536,768]{1,0:T(8,128)(2,1)}) custom-call(bf16[2,4,64,384]{3,2,1,0:T(8,128)(2,1)S(1)} %copy-done.4, bf16[256,1536]{1,0:T(8,128)(2,1)S(1)} %copy-done.3, bf16[256,768]{1,0:T(8,128)(2,1)S(1)} %copy-done.5, f32[1536,768]{1,0:T(8,128)S(1)} %copy-done, ...), custom_call_target="tpu_custom_call" | custom-call | flops 603979776 | bytes 18874368 | tf_op jit(solution)/shard_map/pallas_call | solution.py:503
Async XLA Ops:
  0.6 78.9 %copy-start.1 = (bf16[1536,768]{1,0:T(8,128)(2,1)S(1)}, bf16[1536,768]{1,0:T(8,128)(2,1)}, u32[]{:S(2)}) copy-start(bf16[1536,768]{1,0:T(8,128)(2,1)} %w_ref.1) | copy-start | bytes 7077892
  0.6 78.9 %copy-start.2 = (bf16[1536,768]{1,0:T(8,128)(2,1)S(1)}, bf16[1536,768]{1,0:T(8,128)(2,1)}, u32[]{:S(2)}) copy-start(bf16[1536,768]{1,0:T(8,128)(2,1)} %m_ref.1) | copy-start | bytes 7077892
  79.6 2.3 %copy-start = (f32[1536,768]{1,0:T(8,128)S(1)}, f32[1536,768]{1,0:T(8,128)}, u32[]{:S(2)}) copy-start(f32[1536,768]{1,0:T(8,128)} %get-tuple-element.13.sum_ref) | copy-start | bytes 14155780
  81.9 1.1 %copy-start.3 = (bf16[256,1536]{1,0:T(8,128)(2,1)S(1)}, bf16[256,1536]{1,0:T(8,128)(2,1)}, u32[]{:S(2)}) copy-start(bf16[256,1536]{1,0:T(8,128)(2,1)} %get-tuple-element.11.tok_ref) | copy-start | bytes 2359300
  83.0 1.0 %copy-start.4 = (bf16[2,4,64,384]{3,2,1,0:T(8,128)(2,1)S(1)}, bf16[2,4,64,384]{3,2,1,0:T(8,128)(2,1)}, u32[]{:S(2)}) copy-start(bf16[2,4,64,384]{3,2,1,0:T(8,128)(2,1)} %get-tuple-element.10.act_in) | copy-start | bytes 1179652
  84.0 1.0 %copy-start.5 = (bf16[256,768]{1,0:T(8,128)(2,1)S(1)}, bf16[256,768]{1,0:T(8,128)(2,1)}, u32[]{:S(2)}) copy-start(bf16[256,768]{1,0:T(8,128)(2,1)} %get-tuple-element.12.grad_ref) | copy-start | bytes 1179652

commit v4 on v3

--- a/solution.py
+++ b/solution.py
@@ -30,11 +30,11 @@
 MESH = pl.DeviceIdType.MESH
 
 ORDER = (
-    "start", "bfar", "bz10", "az2", "ay1", "af0", "ay7", "u0", "bz11", "bz20", "af1", "az3", "ay2", "uz1", "f0", "s0",
-    "bz21", "af7", "ay6", "f1", "bz30", "s1", "af2", "m0", "az4", "ay3", "f7", "s7", "af6", "ay5", "m1", "p0", "bz31",
-    "f2", "af3", "b0", "f6", "m7", "p1", "s2", "vz0", "s6", "af5", "ay4", "uz2", "b1", "bz4", "f3", "p7", "f5", "m2",
-    "s3", "b7", "af4", "s5", "m6", "p2", "f4", "b2", "s4", "m3", "vz1", "m5", "vz3", "vz2", "p6", "b6", "m4", "vz4",
-    "p3", "b3", "p5", "vx", "p4", "b5", "fin",
+    "start", "bz10", "bfar", "ay1", "az2", "af0", "ay7", "u0", "bz11", "bz20", "af1", "ay2", "az3", "uz1", "f0", "s0",
+    "bz21", "af7", "ay6", "f1", "bz30", "s1", "af2", "m0", "az4", "ay3", "f7", "s7", "af6", "ay5", "r0", "m1", "f2",
+    "m7", "af3", "p0", "vz0", "bz31", "r1", "f6", "s2", "b0", "s6", "af5", "ay4", "r7", "p1", "uz2", "b1", "bz4",
+    "f3", "m2", "f5", "m6", "p7", "s3", "af4", "s5", "r2", "b7", "r6", "f4", "m3", "vz1", "s4", "m5", "vz3", "p2",
+    "vz2", "p6", "r3", "b2", "b6", "m4", "vz4", "r5", "p3", "vp", "b3", "r4", "p5", "vq", "b5", "p4", "fin",
 )
 
 
@@ -213,7 +213,7 @@
 
     def act_along_z(delta):
         if delta == 0:
-            pltpu.make_async_copy(val2.at[0], val1.at[col], act_sem.at[0]).start()
+            act_stay.start()
         else:
             send(("vz", delta), val2.at[delta], val1.at[col], col_to(delta))
 
@@ -226,17 +226,23 @@
     def act_half_from_z(odd, name):
         arrive((name, 2), val1.at[lax.rem(col + 2, 4), odd])
 
-    def act_along_x():
-        pltpu.make_async_copy(val2.at[0], val1.at[col], act_sem.at[0]).wait()
+    def act_along_x(odd, name):
         for k in (1, 2, 3):
             there = lax.rem(x + k, 4)
-            send(("vx", k), val1.at[there], act_hbm.at[:, home_row(x, there)], x_to(k))
-        pltpu.make_async_copy(val1.at[x], act_hbm.at[:, home_row(x, x)], act_sem.at[1]).start()
+            send((name, k), val1.at[there, odd], act_hbm.at[odd, home_row(x, there)], x_to(k))
+
+    act_stay = pltpu.make_async_copy(val2.at[0], val1.at[col], act_sem.at[0])
+    act_here = pltpu.make_async_copy(val1.at[x], act_hbm.at[:, home_row(x, x)], act_sem.at[1])
+
+    def act_late():
+        act_along_x(zlo, "vq")
+        act_here.start()
 
     def act_done():
-        pltpu.make_async_copy(val1.at[x], act_hbm.at[:, home_row(x, x)], act_sem.at[1]).wait()
-        for k in (1, 2, 3):
-            arrive(("vx", k), act_hbm.at[:, home_row(lax.rem(x + 4 - k, 4), x)])
+        act_here.wait()
+        for odd, name in ((1 - zlo, "vp"), (zlo, "vq")):
+            for k in (1, 2, 3):
+                arrive((name, k), act_hbm.at[odd, home_row(lax.rem(x + 4 - k, 4), x)])
 
     def delta_of(dz):
         return lax.rem((zlo + dz) // 2, 4)
@@ -276,8 +282,22 @@
         delta, odd = delta_of(dz), lax.rem(zlo + dz, 2)
         val2[delta, odd] = gelu_value.astype(jnp.bfloat16)
         grads[dz, 0, chunk, :] = (up2[delta, odd].astype(jnp.float32) * gelu_slope).astype(jnp.bfloat16)
-        for k in (1, 2, 3):
+        for k in (1, 3):
             send(("grad", dz, k), grads.at[dz, 0, chunk], grads.at[dz, 0, chunk], x_to(k))
+
+    def half_chunk(dz, x_of, lo):
+        dy = lax.rem(x_of + delta_of(dz), 4)
+        return pl.ds(pl.multiple_of(dy * TOK + lo, 32), 32)
+
+    def relay(dz):
+        low, high = half_chunk(dz, lax.rem(x + 3, 4), 0), half_chunk(dz, lax.rem(x + 1, 4), 32)
+        send(("far", dz, 1), grads.at[dz, 0, low], grads.at[dz, 0, low], x_to(1))
+        send(("far", dz, 3), grads.at[dz, 0, high], grads.at[dz, 0, high], x_to(3))
+
+    def far_from(dz):
+        far = lax.rem(x + 2, 4)
+        arrive(("far", dz, 1), grads.at[dz, 0, half_chunk(dz, far, 0)])
+        arrive(("far", dz, 3), grads.at[dz, 0, half_chunk(dz, far, 32)])
 
     def pass_on(dz):
         send(("both", dz), grads.at[dz, 0], grads.at[dz, 1], partner)
@@ -339,7 +359,7 @@
             arrive(("sum", dz, k), share.at[dz, k - 1])
 
     def grads_from(dz):
-        for k in (1, 2, 3):
+        for k in (1, 3):
             arrive(("grad", dz, k), grads.at[dz, 0, chunk_rows(dz, lax.rem(x + 4 - k, 4))])
 
     def wait_all(copies):
@@ -360,7 +380,8 @@
         received[f"af{dz}"] = functools.partial(a_from_far, dz)
         received[f"pair{dz}"] = functools.partial(lambda d: arrive(("pair", d), got.at[d]), dz)
         received[f"sum{dz}"] = functools.partial(sums_from, dz)
-        received[f"grad{dz}"] = functools.partial(grads_from, dz)
+        received[f"near{dz}"] = functools.partial(grads_from, dz)
+        received[f"grad{dz}"] = functools.partial(far_from, dz)
         received[f"both{dz}"] = functools.partial(lambda d: arrive(("both", d), grads.at[d, 1]), dz)
     for delta in (1, 2, 3):
         received[f"vz{delta}"] = functools.partial(act_from_z, delta)
@@ -380,7 +401,8 @@
         "u0": (("ux",), stay.start),
         "uz1": (("ux", "az2"), lambda: up_along_z((1, 3))),
         "uz2": (("ux", "az4"), lambda: up_along_z((2,))),
-        "vx": (("vz1", "vz2", "vz3", "vz4"), act_along_x),
+        "vp": (("vz0", "vz1", "vz2", "vz3"), lambda: act_along_x(1 - zlo, "vp")),
+        "vq": (("vz4",), act_late),
         "fin": (("both4",), finish),
     }
     for k in (2, 3, 4):
@@ -399,6 +421,7 @@
         events[f"f{dz}"] = (("w", f"af{dz}") + lower, functools.partial(forward, dz))
         events[f"s{dz}"] = ((f"pair{dz}",), functools.partial(scatter, dz))
         events[f"m{dz}"] = ((f"sum{dz}",) + upper, functools.partial(middle, dz))
+        events[f"r{dz}"] = ((f"near{dz}",), functools.partial(relay, dz))
         events[f"p{dz}"] = ((f"grad{dz}",), functools.partial(pass_on, dz))
         events[f"b{dz}"] = ((f"both{dz}",), functools.partial(backward, dz))
     events["f4"] = (events["f4"][0], forward_last)
@@ -406,6 +429,7 @@
         events[f"vz{delta}"] = ((), functools.partial(act_along_z, delta))
     events["vz2"] = ((), functools.partial(act_half_along_z, 1 - zlo, "va"))
     events["vz4"] = ((), functools.partial(act_half_along_z, zlo, "vb"))
+    received["vz0"] = act_stay.wait
     received["vz2"] = functools.partial(act_half_from_z, 1 - zlo, "va")
     received["vz4"] = functools.partial(act_half_from_z, zlo, "vb")
 
@@ -514,7 +538,7 @@
         ],
         out_specs=(any_space, tile, tile),
         scratch_shapes=[pltpu.SemaphoreType.DMA],
-        compiler_params=pltpu.CompilerParams(vmem_limit_bytes=24 * 1024 * 1024),
+        compiler_params=pltpu.CompilerParams(vmem_limit_bytes=58 * 1024 * 1024),
         cost_estimate=pl.CostEstimate(
             flops=2 * PIECE * FEAT * HID, bytes_accessed=16 * FEAT * HID, transcendentals=FEAT * HID
         ),

time: 90.5 us -> 94.2 us (1.041)
  Pallas kernels: 84.1 us -> 93.4 us
  local copies, waits for them, and re-layouts: 5.46 us -> 0 us
    pallas_call x1, Pallas kernels: 5.17 us -> 15.7 us  [shards(): pl.pallas_call(update, out_shape=(act_shape, block_shape, block_shape), g...]
    unnamed x12 -> x0, local copies, waits for them, and re-layouts: 5.46 us -> none
    pallas_call x1, Pallas kernels: 78.9 us -> 77.6 us  [shards(): pl.pallas_call(kernel, out_shape=(act_shape, jax.ShapeDtypeStruct((FEAT,...]
where the time goes in v4:
time: 94.2 us; the launch traced here: 94 us
  Pallas kernels  93.4 us (99%)
    pallas_call x1, Pallas kernels, shards(): pl.pallas_call(kernel, out_shape=(act_shape, jax.ShapeDtypeStruct((FEAT,...  77.6 us
    pallas_call x1, Pallas kernels, shards(): pl.pallas_call(update, out_shape=(act_shape, block_shape, block_shape), g...  15.7 us

profile of v4, /device:TPU:1, one launch (start us, length us, event | category | flops | bytes accessed | tf_op | source)
XLA Modules:
  0.0 94.0 jit_solution(7496321290307812837)
XLA Ops:
  0.6 77.6 %shard_map.67 = (bf16[2,4,64,384]{3,2,1,0:T(8,128)(2,1)}, f32[1536,768]{1,0:T(8,128)}, bf16[256,1536]{1,0:T(8,128)(2,1)}, bf16[256,768]{1,0:T(8,128)(2,1)}) custom-call(bf16[64,1536]{1,0:T(8,128)(2,1)} %tok_hbm.1, bf16[1536,768]{1,0:T(8,128)(2,1)} %w_ref.1, bf16[2,4,64,384]{3,2,1,0:T(8,128)(2,1)} %bitcast.2), custom_call_target="tpu_custom_call" | custom-call | flops 9663676416 | bytes 12582912 | tf_op jit(solution)/shard_map/pallas_call | solution.py:487
  78.3 15.7 %shard_map.68 = (bf16[2,4,64,384]{3,2,1,0:T(8,128)(2,1)}, bf16[1536,768]{1,0:T(8,128)(2,1)}, bf16[1536,768]{1,0:T(8,128)(2,1)}) custom-call(bf16[2,4,64,384]{3,2,1,0:T(8,128)(2,1)} %get-tuple-element.10.act_in, bf16[256,1536]{1,0:T(8,128)(2,1)} %get-tuple-element.11.tok_ref, bf16[256,768]{1,0:T(8,128)(2,1)} %get-tuple-element.12.grad_ref, ...), custom_call_target="tpu_custom_call" | custom-call | flops 603979776 | bytes 18874368 | tf_op jit(solution)/shard_map/pallas_call | solution.py:527

commit v5 on v4

--- a/solution.py
+++ b/solution.py
@@ -517,7 +517,7 @@
             pltpu.SemaphoreType.DMA((4,)),
         ],
         compiler_params=pltpu.CompilerParams(
-            collective_id=0, has_side_effects=True, vmem_limit_bytes=58 * 1024 * 1024
+            collective_id=0, has_side_effects=True, vmem_limit_bytes=44 * 1024 * 1024
         ),
         cost_estimate=pl.CostEstimate(
             flops=4 * 2048 * FEAT * HID, bytes_accessed=12 * 1024 * 1024, transcendentals=2 * FEAT * HID
@@ -538,7 +538,7 @@
         ],
         out_specs=(any_space, tile, tile),
         scratch_shapes=[pltpu.SemaphoreType.DMA],
-        compiler_params=pltpu.CompilerParams(vmem_limit_bytes=58 * 1024 * 1024),
+        compiler_params=pltpu.CompilerParams(vmem_limit_bytes=16 * 1024 * 1024),
         cost_estimate=pl.CostEstimate(
             flops=2 * PIECE * FEAT * HID, bytes_accessed=16 * FEAT * HID, transcendentals=FEAT * HID
         ),

time: 94.2 us -> 87.9 us (0.933)
  Pallas kernels: 93.4 us -> 83.4 us
  local copies, waits for them, and re-layouts: 0 us -> 3.58 us
    pallas_call x1, Pallas kernels: 15.7 us -> 5.21 us  [shards(): pl.pallas_call(update, out_shape=(act_shape, block_shape, block_shape), g...]
    unnamed x0 -> x8, local copies, waits for them, and re-layouts: none -> 3.58 us
where the time goes in v5:
time: 87.9 us; the launch traced here: 87.7 us
  Pallas kernels  83.4 us (95%)
  local copies, waits for them, and re-layouts  3.58 us (4%)
    pallas_call x1, Pallas kernels, shards(): pl.pallas_call(kernel, out_shape=(act_shape, jax.ShapeDtypeStruct((FEAT,...  78.2 us
    pallas_call x1, Pallas kernels, shards(): pl.pallas_call(update, out_shape=(act_shape, block_shape, block_shape), g...  5.21 us
    unnamed x8, local copies, waits for them, and re-layouts  3.58 us

profile of v5, /device:TPU:1, one launch (start us, length us, event | category | flops | bytes accessed | tf_op | source)
XLA Modules:
  0.0 87.7 jit_solution(1479972944398529003)
XLA Ops:
  0.6 0.0 copy-start
  0.6 1.7 %copy-done = bf16[1536,768]{1,0:T(8,128)(2,1)S(1)} copy-done((bf16[1536,768]{1,0:T(8,128)(2,1)S(1)}, bf16[1536,768]{1,0:T(8,128)(2,1)}, u32[]{:S(2)}) %copy-start) | copy-done | bytes 2359320
  2.3 0.0 copy-start.2
  2.3 1.0 %copy-done.2 = bf16[8,64,384]{2,1,0:T(8,128)(2,1)S(1)} copy-done((bf16[8,64,384]{2,1,0:T(8,128)(2,1)S(1)}, bf16[8,64,384]{2,1,0:T(8,128)(2,1)}, u32[]{:S(2)}) %copy-start.2) | copy-done | bytes 393240
  3.3 0.0 copy-start.3
  3.3 0.9 %copy-done.3 = bf16[64,1536]{1,0:T(8,128)(2,1)S(1)} copy-done((bf16[64,1536]{1,0:T(8,128)(2,1)S(1)}, bf16[64,1536]{1,0:T(8,128)(2,1)}, u32[]{:S(2)}) %copy-start.3) | copy-done | bytes 196632
  4.2 0.0 copy-start.1
  4.2 78.2 %shard_map.67 = (bf16[2,4,64,384]{3,2,1,0:T(8,128)(2,1)S(1)}, f32[1536,768]{1,0:T(8,128)S(1)}, bf16[256,1536]{1,0:T(8,128)(2,1)S(1)}, bf16[256,768]{1,0:T(8,128)(2,1)S(1)}) custom-call(bf16[64,1536]{1,0:T(8,128)(2,1)S(1)} %copy-done.3, bf16[1536,768]{1,0:T(8,128)(2,1)S(1)} %copy-done, bf16[2,4,64,384]{3,2,1,0:T(8,128)(2,1)S(1)} %bitcast.2), custom_call_target="tpu_custom_call" | custom-call | flops 9663676416 | bytes 12582912 | tf_op jit(solution)/shard_map/pallas_call | solution.py:487
  82.5 0.0 copy-done.1
  82.5 5.2 %shard_map.68 = (bf16[2,4,64,384]{3,2,1,0:T(8,128)(2,1)}, bf16[1536,768]{1,0:T(8,128)(2,1)}, bf16[1536,768]{1,0:T(8,128)(2,1)}) custom-call(bf16[2,4,64,384]{3,2,1,0:T(8,128)(2,1)S(1)} %get-tuple-element.10.act_in, bf16[256,1536]{1,0:T(8,128)(2,1)S(1)} %get-tuple-element.11.tok_ref, bf16[256,768]{1,0:T(8,128)(2,1)S(1)} %get-tuple-element.12.grad_ref, ...), custom_call_target="tpu_custom_call" | custom-call | flops 603979776 | bytes 18874368 | tf_op jit(solution)/shard_map/pallas_call | solution.py:527
Async XLA Ops:
  0.6 1.7 %copy-start = (bf16[1536,768]{1,0:T(8,128)(2,1)S(1)}, bf16[1536,768]{1,0:T(8,128)(2,1)}, u32[]{:S(2)}) copy-start(bf16[1536,768]{1,0:T(8,128)(2,1)} %w_ref.1) | copy-start | bytes 7077892
  2.3 1.0 %copy-start.2 = (bf16[8,64,384]{2,1,0:T(8,128)(2,1)S(1)}, bf16[8,64,384]{2,1,0:T(8,128)(2,1)}, u32[]{:S(2)}) copy-start(bf16[8,64,384]{2,1,0:T(8,128)(2,1)} %param.7) | copy-start | bytes 1179652
  3.3 0.9 %copy-start.3 = (bf16[64,1536]{1,0:T(8,128)(2,1)S(1)}, bf16[64,1536]{1,0:T(8,128)(2,1)}, u32[]{:S(2)}) copy-start(bf16[64,1536]{1,0:T(8,128)(2,1)} %tok_hbm.1) | copy-start | bytes 589828
  4.2 78.3 %copy-start.1 = (bf16[1536,768]{1,0:T(8,128)(2,1)S(1)}, bf16[1536,768]{1,0:T(8,128)(2,1)}, u32[]{:S(2)}) copy-start(bf16[1536,768]{1,0:T(8,128)(2,1)} %m_ref.1) | copy-start | bytes 7077892

commit v6 on v5

--- a/solution.py
+++ b/solution.py
@@ -30,11 +30,11 @@
 MESH = pl.DeviceIdType.MESH
 
 ORDER = (
-    "start", "bz10", "bfar", "ay1", "az2", "af0", "ay7", "u0", "bz11", "bz20", "af1", "ay2", "az3", "uz1", "f0", "s0",
-    "bz21", "af7", "ay6", "f1", "bz30", "s1", "af2", "m0", "az4", "ay3", "f7", "s7", "af6", "ay5", "r0", "m1", "f2",
-    "m7", "af3", "p0", "vz0", "bz31", "r1", "f6", "s2", "b0", "s6", "af5", "ay4", "r7", "p1", "uz2", "b1", "bz4",
-    "f3", "m2", "f5", "m6", "p7", "s3", "af4", "s5", "r2", "b7", "r6", "f4", "m3", "vz1", "s4", "m5", "vz3", "p2",
-    "vz2", "p6", "r3", "b2", "b6", "m4", "vz4", "r5", "p3", "vp", "b3", "r4", "p5", "vq", "b5", "p4", "fin",
+    "start", "bfar", "bz10", "ay1", "az2", "af0", "ay7", "u0", "bz11", "bz20", "af1", "az3", "uz1", "ay2", "f0",
+    "bz21", "af7", "ay6", "s0", "f1", "bz30", "af2", "s1", "m0", "az4", "ay3", "f7", "af6", "ay5", "s7", "r0", "m1",
+    "bz31", "af3", "f2", "f6", "m7", "p0", "vz0", "r1", "s2", "uz2", "af5", "ay4", "s6", "b0", "r7", "p1", "bz4",
+    "f3", "f5", "b1", "m2", "s3", "af4", "s5", "m6", "p7", "r2", "b7", "f4", "m3", "vz1", "s4", "m5", "vz3", "vz2",
+    "r6", "p2", "r3", "b2", "m4", "vz4", "r5", "p6", "p3", "vp", "b6", "r4", "b3", "p5", "vq", "p4", "b5", "fin",
 )
 
 

time: 87.9 us -> 88.8 us (1.010); the launches traced: 87.7 us -> 87.6 us
  no operation moved by 1% of the time
where the time goes in v6:
time: 88.8 us; the launch traced here: 87.6 us
  Pallas kernels  83.4 us (94%)
  local copies, waits for them, and re-layouts  3.58 us (4%)
    pallas_call x1, Pallas kernels, shards(): pl.pallas_call(kernel, out_shape=(act_shape, jax.ShapeDtypeStruct((FEAT,...  78.2 us
    pallas_call x1, Pallas kernels, shards(): pl.pallas_call(update, out_shape=(act_shape, block_shape, block_shape), g...  5.2 us
    unnamed x8, local copies, waits for them, and re-layouts  3.58 us

profile of v6, /device:TPU:1, one launch (start us, length us, event | category | flops | bytes accessed | tf_op | source)
XLA Modules:
  0.0 87.6 jit_solution(241108851148025181)
XLA Ops:
  0.6 0.0 copy-start
  0.6 1.7 %copy-done = bf16[1536,768]{1,0:T(8,128)(2,1)S(1)} copy-done((bf16[1536,768]{1,0:T(8,128)(2,1)S(1)}, bf16[1536,768]{1,0:T(8,128)(2,1)}, u32[]{:S(2)}) %copy-start) | copy-done | bytes 2359320
  2.3 0.0 copy-start.2
  2.3 1.0 %copy-done.2 = bf16[8,64,384]{2,1,0:T(8,128)(2,1)S(1)} copy-done((bf16[8,64,384]{2,1,0:T(8,128)(2,1)S(1)}, bf16[8,64,384]{2,1,0:T(8,128)(2,1)}, u32[]{:S(2)}) %copy-start.2) | copy-done | bytes 393240
  3.3 0.0 copy-start.3
  3.3 0.9 %copy-done.3 = bf16[64,1536]{1,0:T(8,128)(2,1)S(1)} copy-done((bf16[64,1536]{1,0:T(8,128)(2,1)S(1)}, bf16[64,1536]{1,0:T(8,128)(2,1)}, u32[]{:S(2)}) %copy-start.3) | copy-done | bytes 196632
  4.2 0.0 copy-start.1
  4.2 78.2 %shard_map.67 = (bf16[2,4,64,384]{3,2,1,0:T(8,128)(2,1)S(1)}, f32[1536,768]{1,0:T(8,128)S(1)}, bf16[256,1536]{1,0:T(8,128)(2,1)S(1)}, bf16[256,768]{1,0:T(8,128)(2,1)S(1)}) custom-call(bf16[64,1536]{1,0:T(8,128)(2,1)S(1)} %copy-done.3, bf16[1536,768]{1,0:T(8,128)(2,1)S(1)} %copy-done, bf16[2,4,64,384]{3,2,1,0:T(8,128)(2,1)S(1)} %bitcast.2), custom_call_target="tpu_custom_call" | custom-call | flops 9663676416 | bytes 12582912 | tf_op jit(solution)/shard_map/pallas_call | solution.py:487
  82.4 0.0 copy-done.1
  82.4 5.2 %shard_map.68 = (bf16[2,4,64,384]{3,2,1,0:T(8,128)(2,1)}, bf16[1536,768]{1,0:T(8,128)(2,1)}, bf16[1536,768]{1,0:T(8,128)(2,1)}) custom-call(bf16[2,4,64,384]{3,2,1,0:T(8,128)(2,1)S(1)} %get-tuple-element.10.act_in, bf16[256,1536]{1,0:T(8,128)(2,1)S(1)} %get-tuple-element.11.tok_ref, bf16[256,768]{1,0:T(8,128)(2,1)S(1)} %get-tuple-element.12.grad_ref, ...), custom_call_target="tpu_custom_call" | custom-call | flops 603979776 | bytes 18874368 | tf_op jit(solution)/shard_map/pallas_call | solution.py:527
Async XLA Ops:
  0.6 1.7 %copy-start = (bf16[1536,768]{1,0:T(8,128)(2,1)S(1)}, bf16[1536,768]{1,0:T(8,128)(2,1)}, u32[]{:S(2)}) copy-start(bf16[1536,768]{1,0:T(8,128)(2,1)} %w_ref.1) | copy-start | bytes 7077892
  2.3 1.0 %copy-start.2 = (bf16[8,64,384]{2,1,0:T(8,128)(2,1)S(1)}, bf16[8,64,384]{2,1,0:T(8,128)(2,1)}, u32[]{:S(2)}) copy-start(bf16[8,64,384]{2,1,0:T(8,128)(2,1)} %param.7) | copy-start | bytes 1179652
  3.3 0.9 %copy-start.3 = (bf16[64,1536]{1,0:T(8,128)(2,1)S(1)}, bf16[64,1536]{1,0:T(8,128)(2,1)}, u32[]{:S(2)}) copy-start(bf16[64,1536]{1,0:T(8,128)(2,1)} %tok_hbm.1) | copy-start | bytes 589828
  4.2 78.2 %copy-start.1 = (bf16[1536,768]{1,0:T(8,128)(2,1)S(1)}, bf16[1536,768]{1,0:T(8,128)(2,1)}, u32[]{:S(2)}) copy-start(bf16[1536,768]{1,0:T(8,128)(2,1)} %m_ref.1) | copy-start | bytes 7077892

commit v7 on v6

--- a/solution.py
+++ b/solution.py
@@ -30,11 +30,11 @@
 MESH = pl.DeviceIdType.MESH
 
 ORDER = (
-    "start", "bfar", "bz10", "ay1", "az2", "af0", "ay7", "u0", "bz11", "bz20", "af1", "az3", "uz1", "ay2", "f0",
-    "bz21", "af7", "ay6", "s0", "f1", "bz30", "af2", "s1", "m0", "az4", "ay3", "f7", "af6", "ay5", "s7", "r0", "m1",
-    "bz31", "af3", "f2", "f6", "m7", "p0", "vz0", "r1", "s2", "uz2", "af5", "ay4", "s6", "b0", "r7", "p1", "bz4",
-    "f3", "f5", "b1", "m2", "s3", "af4", "s5", "m6", "p7", "r2", "b7", "f4", "m3", "vz1", "s4", "m5", "vz3", "vz2",
-    "r6", "p2", "r3", "b2", "m4", "vz4", "r5", "p6", "p3", "vp", "b6", "r4", "b3", "p5", "vq", "p4", "b5", "fin",
+    "start", "bfar", "bz10", "ay7", "az2", "ay1", "u0", "af0", "bz11", "bz20", "af7", "az3", "uz1", "ay2", "af1",
+    "ay6", "bz21", "f0", "f7", "s0", "bz30", "s7", "af2", "ay3", "az4", "ay5", "f1", "m0", "s1", "af6", "m7", "r0",
+    "bz31", "f2", "af3", "m1", "r7", "vz0", "p0", "s2", "af5", "b0", "f6", "ay4", "uz2", "p7", "r1", "bz4", "s6",
+    "f3", "f5", "m2", "b7", "af4", "s3", "p1", "s5", "m6", "b1", "r2", "f4", "m3", "vz1", "s4", "m5", "vz3", "vz2",
+    "r6", "p2", "r3", "b2", "m4", "vz4", "r5", "p6", "p3", "vp", "b6", "r4", "b3", "vq", "p5", "p4", "b5", "fin",
 )
 
 

time: 88.8 us -> 87.2 us (0.982); the launches traced: 87.6 us -> 87.1 us
  no operation moved by 1% of the time
where the time goes in v7:
time: 87.2 us; the launch traced here: 87.1 us
  Pallas kernels  82.8 us (95%)
  local copies, waits for them, and re-layouts  3.58 us (4%)
    pallas_call x1, Pallas kernels, shards(): pl.pallas_call(kernel, out_shape=(act_shape, jax.ShapeDtypeStruct((FEAT,...  77.6 us
    pallas_call x1, Pallas kernels, shards(): pl.pallas_call(update, out_shape=(act_shape, block_shape, block_shape), g...  5.2 us
    unnamed x8, local copies, waits for them, and re-layouts  3.58 us

profile of v7, /device:TPU:1, one launch (start us, length us, event | category | flops | bytes accessed | tf_op | source)
XLA Modules:
  0.0 87.1 jit_solution(16782054627865849549)
XLA Ops:
  0.6 0.0 copy-start
  0.6 1.7 %copy-done = bf16[1536,768]{1,0:T(8,128)(2,1)S(1)} copy-done((bf16[1536,768]{1,0:T(8,128)(2,1)S(1)}, bf16[1536,768]{1,0:T(8,128)(2,1)}, u32[]{:S(2)}) %copy-start) | copy-done | bytes 2359320
  2.3 0.0 copy-start.2
  2.3 1.0 %copy-done.2 = bf16[8,64,384]{2,1,0:T(8,128)(2,1)S(1)} copy-done((bf16[8,64,384]{2,1,0:T(8,128)(2,1)S(1)}, bf16[8,64,384]{2,1,0:T(8,128)(2,1)}, u32[]{:S(2)}) %copy-start.2) | copy-done | bytes 393240
  3.3 0.0 copy-start.3
  3.3 0.9 %copy-done.3 = bf16[64,1536]{1,0:T(8,128)(2,1)S(1)} copy-done((bf16[64,1536]{1,0:T(8,128)(2,1)S(1)}, bf16[64,1536]{1,0:T(8,128)(2,1)}, u32[]{:S(2)}) %copy-start.3) | copy-done | bytes 196632
  4.2 0.0 copy-start.1
  4.2 77.6 %shard_map.67 = (bf16[2,4,64,384]{3,2,1,0:T(8,128)(2,1)S(1)}, f32[1536,768]{1,0:T(8,128)S(1)}, bf16[256,1536]{1,0:T(8,128)(2,1)S(1)}, bf16[256,768]{1,0:T(8,128)(2,1)S(1)}) custom-call(bf16[64,1536]{1,0:T(8,128)(2,1)S(1)} %copy-done.3, bf16[1536,768]{1,0:T(8,128)(2,1)S(1)} %copy-done, bf16[2,4,64,384]{3,2,1,0:T(8,128)(2,1)S(1)} %bitcast.2), custom_call_target="tpu_custom_call" | custom-call | flops 9663676416 | bytes 12582912 | tf_op jit(solution)/shard_map/pallas_call | solution.py:487
  81.9 0.0 copy-done.1
  81.9 5.2 %shard_map.68 = (bf16[2,4,64,384]{3,2,1,0:T(8,128)(2,1)}, bf16[1536,768]{1,0:T(8,128)(2,1)}, bf16[1536,768]{1,0:T(8,128)(2,1)}) custom-call(bf16[2,4,64,384]{3,2,1,0:T(8,128)(2,1)S(1)} %get-tuple-element.10.act_in, bf16[256,1536]{1,0:T(8,128)(2,1)S(1)} %get-tuple-element.11.tok_ref, bf16[256,768]{1,0:T(8,128)(2,1)S(1)} %get-tuple-element.12.grad_ref, ...), custom_call_target="tpu_custom_call" | custom-call | flops 603979776 | bytes 18874368 | tf_op jit(solution)/shard_map/pallas_call | solution.py:527
Async XLA Ops:
  0.6 1.7 %copy-start = (bf16[1536,768]{1,0:T(8,128)(2,1)S(1)}, bf16[1536,768]{1,0:T(8,128)(2,1)}, u32[]{:S(2)}) copy-start(bf16[1536,768]{1,0:T(8,128)(2,1)} %w_ref.1) | copy-start | bytes 7077892
  2.3 1.0 %copy-start.2 = (bf16[8,64,384]{2,1,0:T(8,128)(2,1)S(1)}, bf16[8,64,384]{2,1,0:T(8,128)(2,1)}, u32[]{:S(2)}) copy-start(bf16[8,64,384]{2,1,0:T(8,128)(2,1)} %param.7) | copy-start | bytes 1179652
  3.3 0.9 %copy-start.3 = (bf16[64,1536]{1,0:T(8,128)(2,1)S(1)}, bf16[64,1536]{1,0:T(8,128)(2,1)}, u32[]{:S(2)}) copy-start(bf16[64,1536]{1,0:T(8,128)(2,1)} %tok_hbm.1) | copy-start | bytes 589828
  4.2 77.6 %copy-start.1 = (bf16[1536,768]{1,0:T(8,128)(2,1)S(1)}, bf16[1536,768]{1,0:T(8,128)(2,1)}, u32[]{:S(2)}) copy-start(bf16[1536,768]{1,0:T(8,128)(2,1)} %m_ref.1) | copy-start | bytes 7077892
